TPU v7x, 32 devices: a whole 2x2x4 slice. The times are simulated.
32 devices in a mesh: section: 4 (over z), dp: 2 (over x), seq: 4 (over y, core).
Axes of the slice: x: 2, y: 2, z: 4, core: 2. Of those that a mesh axis runs over, the one named last changes fastest.
Arguments:
- incoming: bfloat16 [4, 2, 512, 4096], P('section', 'dp', 'seq'), may hold values from -6 to 6
- chosen: int32 [4, 2, 64], P('section', 'dp'), may hold values from 0 to 511, as said below
- norm_gain: float32 [4, 4096], P('section'), may hold values from 0.1 to 1.9
- router: bfloat16 [4, 4096], P('section'), may hold values from -0.25 to 0.25
- w_query: bfloat16 [4, 4096, 4096], P('section', 'dp', 'seq'), may hold values from -1 to 1
- w_key: bfloat16 [4, 4096, 4096], P('section', 'dp', 'seq'), may hold values from -1 to 1
- w_value: bfloat16 [4, 4096, 4096], P('section', 'dp', 'seq'), may hold values from -0.09375 to 0.09375
- w_out_t: bfloat16 [4, 4096, 4096], P('section', 'dp', 'seq'), may hold values from -0.5 to 0.5
Outputs:
- outgoing: bfloat16 [4, 2, 512, 4096], P('section', 'dp', 'seq')
Inputs may be any that keep to these rules, and one draw needn't show every extreme that they name: chosen[s, b] holds 64 distinct positions in increasing order; each aligned block of 128 positions holds at most 32 of them, and in every sequence one block holds exactly 32.
All inputs are finite; a program needn't handle non-finite values.
Results may differ from a plain program's by a relative error of at most 0.014.
Values may be sent and summed in bfloat16 or wider, within the bound.
A program may use at most 128 MiB of HBM per device.

v0:
```python
import jax
import jax.numpy as jnp
from jax import lax
from jax.sharding import PartitionSpec as P

HD = 128


EPSILON = 1e-05
ROPE_BASE = 500000.0
NEG_FILL = -1e30


def shifted(value, axis, steps):
    count = lax.axis_size(axis)
    pairs = [(source, (source + steps) % count) for source in range(count)]
    return lax.ppermute(value, axis, pairs)


def rms_norm(rows_in, gain_vec):
    widened = rows_in.astype(jnp.float32)
    inv_scale = lax.rsqrt(jnp.mean(widened * widened, axis=-1, keepdims=True) + EPSILON)
    return (widened * inv_scale * gain_vec[None, :]).astype(jnp.bfloat16)


def apply_rope(projected, positions):
    half_dim = HD // 2
    inverse_freq = ROPE_BASE ** (-2.0 * jnp.arange(half_dim, dtype=jnp.float32) / HD)
    angles = positions.astype(jnp.float32)[:, None] * inverse_freq[None, :]
    cosine = jnp.cos(angles)[:, None, :]
    sine_vals = jnp.sin(angles)[:, None, :]
    shaped = projected.reshape(projected.shape[0], -1, HD)
    first_half = shaped[:, :, :half_dim]
    second_half = shaped[:, :, half_dim:]
    rotated = jnp.concatenate(
        [
            first_half * cosine - second_half * sine_vals,
            second_half * cosine + first_half * sine_vals,
        ],
        axis=-1,
    )
    return rotated.reshape(projected.shape)


def attend_rows(joint_proj, positions, key_live, head_width):
    queries = apply_rope(joint_proj[:, :head_width], positions).astype(jnp.bfloat16)
    keys_rot = apply_rope(joint_proj[:, head_width : 2 * head_width], positions).astype(
        jnp.bfloat16
    )
    values_out = joint_proj[:, 2 * head_width :].astype(jnp.bfloat16)
    heads_split = queries.reshape(queries.shape[0], -1, HD)
    keys_split = keys_rot.reshape(keys_rot.shape[0], -1, HD)
    values_split = values_out.reshape(values_out.shape[0], -1, HD)
    scores = jnp.einsum(
        "qhd,khd->hqk", heads_split, keys_split, preferred_element_type=jnp.float32
    ) * HD ** (-0.5)
    allowed = (positions[None, :] <= positions[:, None]) & key_live[None, :]
    scores = jnp.where(allowed[None, :, :], scores, NEG_FILL)
    peak_val = jnp.max(scores, axis=-1, keepdims=True)
    exponent = jnp.exp(scores - peak_val)
    attn_weights = (exponent / jnp.sum(exponent, axis=-1, keepdims=True)).astype(jnp.bfloat16)
    mixed = jnp.einsum(
        "hqk,khd->qhd", attn_weights, values_split, preferred_element_type=jnp.float32
    )
    return mixed.astype(jnp.bfloat16).reshape(queries.shape)


def per_device(incoming, chosen, norm_gain, router, w_query, w_key, w_value, w_out_t):
    arrived = shifted(incoming, "section", 1)
    tokens = arrived[0, 0]
    tok_dev = tokens.shape[0]
    shards = lax.axis_size("seq")
    my_index = lax.axis_index("seq")
    pick_list = chosen[0, 0]
    chosen_count = pick_list.shape[0]
    slot_cap = tok_dev // 4
    seq_length = tok_dev * shards
    owner_of = pick_list // tok_dev
    shard_ids = jnp.arange(shards, dtype=jnp.int32)
    counts = jnp.sum((owner_of[:, None] == shard_ids[None, :]).astype(jnp.int32), axis=0)
    starts = jnp.cumsum(counts) - counts
    padded_list = jnp.concatenate([pick_list, jnp.full((slot_cap,), seq_length, jnp.int32)])
    slot_ids = jnp.arange(slot_cap, dtype=jnp.int32)
    my_start = starts[my_index]
    my_count = counts[my_index]
    my_pos = lax.dynamic_slice_in_dim(padded_list, my_start, slot_cap)
    my_live = slot_ids < my_count
    local_rows = jnp.where(my_live, my_pos - my_index * tok_dev, 0)
    raw_rows = jnp.take(tokens, local_rows, axis=0)
    raw_rows = jnp.where(my_live[:, None], raw_rows, jnp.zeros_like(raw_rows))
    router_gate = jax.nn.sigmoid(jnp.dot(raw_rows, router[0], preferred_element_type=jnp.float32))
    normed = rms_norm(raw_rows, norm_gain[0])
    weights = (
        lax.all_gather(w_query, "dp", axis=1, tiled=True),
        lax.all_gather(w_key, "dp", axis=1, tiled=True),
        lax.all_gather(w_value, "dp", axis=1, tiled=True),
        lax.all_gather(w_out_t, "dp", axis=1, tiled=True),
    )
    w_joint = jnp.concatenate([weights[0][0], weights[1][0], weights[2][0]], axis=1)
    w_back = weights[3][0]
    head_cols = w_back.shape[1]
    slot_live = (slot_ids[None, :] < counts[:, None]).reshape(-1)
    spread = lax.all_to_all(normed, "seq", split_axis=1, concat_axis=0, tiled=True)
    slot_of = jnp.arange(chosen_count, dtype=jnp.int32) - jnp.take(starts, owner_of)
    flat_of = owner_of * slot_cap + slot_of
    compact = jnp.take(spread, flat_of, axis=0)
    joint_proj = jnp.dot(
        lax.all_gather(compact, "seq", axis=1, tiled=True),
        w_joint,
        preferred_element_type=jnp.float32,
    )
    all_live = jnp.ones((chosen_count,), dtype=bool)
    attended = attend_rows(joint_proj, pick_list, all_live, head_cols)
    partial_out = lax.dot_general(
        attended, w_back, (((1,), (1,)), ((), ())), preferred_element_type=jnp.float32
    )
    summed = lax.psum_scatter(
        partial_out.astype(jnp.bfloat16), "seq", scatter_dimension=1, tiled=True
    )
    back_index = jnp.minimum(starts[:, None] + slot_ids[None, :], chosen_count - 1).reshape(-1)
    slotted = jnp.take(summed, back_index, axis=0)
    slotted = jnp.where(slot_live[:, None], slotted, jnp.zeros_like(slotted))
    delta_rows = lax.all_to_all(slotted, "seq", split_axis=0, concat_axis=1, tiled=True)
    updated = (
        raw_rows.astype(jnp.float32) + router_gate[:, None] * delta_rows.astype(jnp.float32)
    ).astype(jnp.bfloat16)
    target = jnp.where(my_live, local_rows, tok_dev)
    result = tokens.at[target].set(updated, mode="drop")
    return result[None, None]


def solution(mesh):
    in_specs = (
        P("section", "dp", "seq", None),
        P("section", "dp", None),
        P("section", None),
        P("section", None),
        P("section", "dp", "seq"),
        P("section", "dp", "seq"),
        P("section", "dp", "seq"),
        P("section", "dp", "seq"),
    )
    out_specs = P("section", "dp", "seq", None)
    return jax.shard_map(
        per_device, mesh=mesh, in_specs=in_specs, out_specs=out_specs, check_vma=False
    )
```

profile of v0, /device:TPU:1, one launch (start us, length us, event | category | flops | bytes accessed | tf_op | source)
XLA Modules:
  0.0 481.6 jit_solution(9968805000226782039)
XLA Ops:
  6.6 0.7 all-gather.5.cloned.1.call-update
  7.3 0.7 all-gather.7.cloned.1.call-update
  8.1 0.7 all-gather.9.cloned.1.call-update
  8.8 0.5 all-gather.11.cloned.1.call-update
  9.3 2.2 collective-permute-start
  11.5 0.1 convert_reduce_fusion
  11.7 0.2 reduce-window.7
  11.8 0.7 dynamic_slice.9
  12.5 0.7 fusion.60
  15.2 0.7 compare_and_fusion.2
  16.0 0.6 compare_select_fusion.6
  16.6 0.6 broadcast.463
  17.2 0.7 reduce.3
  17.9 2.5 compare_and_fusion
  20.5 0.2 multiply_cosine_fusion
  20.7 15.8 %collective-permute-done = bf16[1,1,128,4096]{3,2,1,0:T(8,128)(2,1)S(1)} collective-permute-done((bf16[1,1,128,4096]{3,2,1,0:T(8,128)(2,1)S(1)}, bf16[1,1,128,4096]{3,2,1,0:T(8,128)(2,1)S(1)}, u32[]{:S(2)}, u32[]{:S(2)}) %collective-permute-start) | collective-permute-done | bytes 1048608 | tf_op jit(solution)/shard_map/ppermute | solution.py:17
  36.4 0.7 gather_fusion
  37.1 0.3 fusion.20
  37.4 0.9 multiply_convert_fusion
  38.3 4.6 all-to-all-start
  42.9 0.1 broadcast_compare_fusion
  43.0 5.2 %all-to-all-done = bf16[32,4,1024]{2,0,1:T(8,128)(2,1)S(1)} async-done(((bf16[32,4,1024]{2,0,1:T(8,128)(2,1)}), bf16[32,4,1024]{2,0,1:T(8,128)(2,1)S(1)}, u32[]{:S(2)}, u32[]{:S(2)}) %all-to-all-start) | async-done | bytes 262176 | tf_op jit(solution)/shard_map/all_to_all | solution.py:103
  48.2 0.7 gather_fusion.1
  48.9 0.1 broadcast_select_fusion
  49.0 7.3 %all_gather.15 = bf16[64,4096]{1,0:T(8,128)(2,1)S(1)} all-gather(bf16[64,1024]{1,0:T(8,128)(2,1)S(1)} %broadcast_select_fusion), channel_id=1, replica_groups=mesh['section'=4,'dp'=2,'seq'=4] {'seq'}, dimensions={1}, use_global_device_ids=true | all-gather | bytes 655360 | tf_op jit(solution)/shard_map/all_gather | solution.py:108
  56.3 58.7 %all-gather.5.cloned.1.call-done = bf16[1,4096,1024]{2,1,0:T(8,128)(2,1)} async-done(((bf16[1,2048,1024]{2,1,0:T(8,128)(2,1)}), bf16[1,4096,1024]{2,1,0:T(8,128)(2,1)}) %all-gather.5.cloned.1.call-update) | async-done | bytes 8388624 | tf_op jit(solution)/shard_map/all_gather | solution.py:94
  115.0 105.6 %all-gather.7.cloned.1.call-done = bf16[1,4096,1024]{2,1,0:T(8,128)(2,1)} async-done(((bf16[1,2048,1024]{2,1,0:T(8,128)(2,1)}), bf16[1,4096,1024]{2,1,0:T(8,128)(2,1)}) %all-gather.7.cloned.1.call-update) | async-done | bytes 8388624 | tf_op jit(solution)/shard_map/all_gather | solution.py:95
  220.6 105.6 %all-gather.9.cloned.1.call-done = bf16[1,4096,1024]{2,1,0:T(8,128)(2,1)} async-done(((bf16[1,2048,1024]{2,1,0:T(8,128)(2,1)}), bf16[1,4096,1024]{2,1,0:T(8,128)(2,1)}) %all-gather.9.cloned.1.call-update) | async-done | bytes 8388624 | tf_op jit(solution)/shard_map/all_gather | solution.py:96
  326.2 10.7 %fusion.1 = f32[64,3072]{1,0:T(8,128)S(1)} fusion(bf16[64,4096]{1,0:T(8,128)(2,1)S(1)} %all_gather.15, bf16[4096,1024]{1,0:T(8,128)(2,1)} %bitcast.103, bf16[4096,1024]{1,0:T(8,128)(2,1)} %bitcast.102, bf16[4096,1024]{1,0:T(8,128)(2,1)} %bitcast.101), kind=kOutput, calls=%fused_computation.5 | convolution fusion | flops 1686110208 | bytes 26476544 | tf_op jit(solution)/shard_map/dot_general | solution.py:107
  337.1 0.1 fusion.58
  337.2 0.1 fusion.59
  337.4 0.2 subtract_convert_fusion
  337.6 0.3 fusion.61
  337.9 0.2 fusion.15
  338.2 93.5 %all-gather.11.cloned.1.call-done = bf16[1,4096,1024]{2,1,0:T(8,128)(2,1)} async-done(((bf16[1,2048,1024]{2,1,0:T(8,128)(2,1)}), bf16[1,4096,1024]{2,1,0:T(8,128)(2,1)}) %all-gather.11.cloned.1.call-update) | async-done | bytes 8388624 | tf_op jit(solution)/shard_map/all_gather | solution.py:97
  431.6 6.8 %fusion.9 = bf16[64,4096]{1,0:T(8,128)(2,1)} fusion(bf16[1,4096,1024]{2,1,0:T(8,128)(2,1)} %all-gather.11.cloned.1.call-done, bf16[8,8,8,128]{3,2,1,0:T(8,128)(2,1)S(1)} %fusion.15), kind=kOutput, calls=%fused_computation.13 | convolution fusion | flops 537133056 | bytes 9043968 | tf_op jit(solution)/shard_map/dot_general | solution.py:114
  438.5 0.1 add_minimum_fusion
  438.6 0.1 min.22
  438.7 0.1 compare_and_fusion.1
  438.8 0.1 iota_compare_fusion
  438.8 21.6 %reduce-scatter.2.cloned.1.call-done = bf16[64,1024]{1,0:T(8,128)(2,1)} async-done(((bf16[64,4096]{1,0:T(8,128)(2,1)}), bf16[64,1024]{1,0:T(8,128)(2,1)}) %reduce-scatter.2.cloned.1.call-update) | async-done | bytes 131088 | tf_op jit(solution)/shard_map/reduce_scatter | solution.py:117
  460.4 2.0 gather_fusion.2
  462.4 0.8 select_select_fusion
  463.2 4.0 all-to-all-start.1
  467.2 0.2 fusion.19
  467.4 5.0 %all-to-all-done.1 = bf16[4,32,1024]{2,1,0:T(8,128)(2,1)S(1)} async-done(((bf16[4,32,1024]{2,1,0:T(8,128)(2,1)}), bf16[4,32,1024]{2,1,0:T(8,128)(2,1)S(1)}, u32[]{:S(2)}, u32[]{:S(2)}) %all-to-all-start.1) | async-done | bytes 262176 | tf_op jit(solution)/shard_map/all_to_all | solution.py:123
  472.5 1.6 scatter_custom_fusion
  474.1 1.0 copy.76
  (30 shorter events, 0.5 us)
Async XLA Ops:
  6.5 460.7 %copy-start = (bf16[1,4096]{1,0:T(2,128)(2,1)S(1)}, bf16[1,4096]{1,0:T(2,128)(2,1)}, u32[]{:S(2)}) copy-start(bf16[1,4096]{1,0:T(2,128)(2,1)} %param.11) | copy-start | bytes 24580
  6.5 2.8 copy-start.3
  6.5 5.0 %copy-start.2 = (s32[1,1,64]{2,1,0:T(1,128)S(1)}, s32[1,1,64]{2,1,0:T(1,128)}, u32[]{:S(2)}) copy-start(s32[1,1,64]{2,1,0:T(1,128)} %param.9) | copy-start | bytes 772
  6.5 10.7 %copy-start.1 = (f32[1,4096]{1,0:T(1,128)S(1)}, f32[1,4096]{1,0:T(1,128)}, u32[]{:S(2)}) copy-start(f32[1,4096]{1,0:T(1,128)} %param.10) | copy-start | bytes 49156
  6.5 108.5 %all-gather.5.cloned.1.call-start = ((), (), s32[]{:S(2)}) async-start(), calls=%async_computation.3 | async-start | bytes 12582912 | tf_op jit(solution)/shard_map/all_gather | solution.py:94
  7.3 213.3 %all-gather.7.cloned.1.call-start = ((), (), s32[]{:S(2)}) async-start(), calls=%async_computation.4 | async-start | bytes 12582912 | tf_op jit(solution)/shard_map/all_gather | solution.py:95
  8.0 318.2 %all-gather.9.cloned.1.call-start = ((), (), s32[]{:S(2)}) async-start(), calls=%async_computation.5 | async-start | bytes 12582912 | tf_op jit(solution)/shard_map/all_gather | solution.py:96
  8.8 422.9 %all-gather.11.cloned.1.call-start = ((), (), s32[]{:S(2)}) async-start(), calls=%async_computation.6 | async-start | bytes 12582912 | tf_op jit(solution)/shard_map/all_gather | solution.py:97
  9.3 27.1 %collective-permute-start = (bf16[1,1,128,4096]{3,2,1,0:T(8,128)(2,1)S(1)}, bf16[1,1,128,4096]{3,2,1,0:T(8,128)(2,1)S(1)}, u32[]{:S(2)}, u32[]{:S(2)}) collective-permute-start(bf16[1,1,128,4096]{3,2,1,0:T(8,128)(2,1)S(1)} %copy-done.3), channel_id=1, source_target_pairs={{0,8},{8,16},{16,24},{24,0},{1,9},{9,17},{17,25},{25,1},{2,10},{10... | collective-permute-start | bytes 3145736 | tf_op jit(solution)/shard_map/ppermute | solution.py:17
  38.3 9.9 %all-to-all-start = ((bf16[32,4,1024]{2,0,1:T(8,128)(2,1)}), bf16[32,4,1024]{2,0,1:T(8,128)(2,1)S(1)}, u32[]{:S(2)}, u32[]{:S(2)}) async-start(bf16[32,4,1024]{2,0,1:T(8,128)(2,1)} %multiply_convert_fusion), calls=%async_computation | async-start | bytes 524288 | tf_op jit(solution)/shard_map/all_to_all | solution.py:103
  42.9 417.5 %reduce-scatter.2.cloned.1.call-start = ((), (), s32[]{:S(2)}) async-start(), calls=%async_computation.7 | async-start | bytes 655360 | tf_op jit(solution)/shard_map/reduce_scatter | solution.py:117
  463.2 9.2 %all-to-all-start.1 = ((bf16[4,32,1024]{2,1,0:T(8,128)(2,1)}), bf16[4,32,1024]{2,1,0:T(8,128)(2,1)S(1)}, u32[]{:S(2)}, u32[]{:S(2)}) async-start(bf16[4,32,1024]{2,1,0:T(8,128)(2,1)} %select_select_fusion), calls=%async_computation.2 | async-start | bytes 524288 | tf_op jit(solution)/shard_map/all_to_all | solution.py:123
Sparse Core Ops, SparseCore 0:
  8.9 106.0 all-gather.4
  116.6 104.0 all-gather.6
  222.2 103.9 all-gather.8
  327.6 103.9 all-gather.10
  438.6 21.7 reduce-scatter.1
where the time goes:
time: 483 us; the launch traced here: 482 us
  waiting for transfers between devices  414 us (86%)
  matrix products  18.3 us (4%)
  between operations  15.4 us (3%)
  starting transfers between devices  11 us (2%)
  other arithmetic  9.33 us (2%)
  blocking collectives  7.29 us (2%)
  local copies, waits for them, and re-layouts  6.81 us (1%)
    all_gather x1, waiting for transfers between devices, per_device(): lax.all_gather(w_key, 'dp', axis=1, tiled=True)  106 us
    all_gather x1, waiting for transfers between devices, per_device(): lax.all_gather(w_value, 'dp', axis=1, tiled=True)  106 us
    all_gather x1, waiting for transfers between devices, per_device(): lax.all_gather(w_out_t, 'dp', axis=1, tiled=True)  93.5 us
    all_gather x1, waiting for transfers between devices, per_device(): lax.all_gather(w_query, 'dp', axis=1, tiled=True)  58.7 us
    reduce_scatter x1, waiting for transfers between devices, per_device(): lax.psum_scatter(partial_out.astype(jnp.bfloat16), 'seq', scatter_dimensi...  21.6 us
    ppermute x1, waiting for transfers between devices, shifted(): return lax.ppermute(value, axis, pairs)  15.8 us
    dot_general x1, matrix products, per_device(): jnp.dot(lax.all_gather(compact, 'seq', axis=1, tiled=True), w_joint, pref...  10.7 us
  transfers between devices with their start and end apart: 8, of which 8 were waited for; matrix products, arithmetic and copies ran while one was open for 5% of the time, Pallas kernels for 0%

commit v1 on v0

--- a/solution.py
+++ b/solution.py
@@ -65,65 +65,84 @@
     return mixed.astype(jnp.bfloat16).reshape(queries.shape)
 
 
-def per_device(incoming, chosen, norm_gain, router, w_query, w_key, w_value, w_out_t):
-    arrived = shifted(incoming, "section", 1)
-    tokens = arrived[0, 0]
-    tok_dev = tokens.shape[0]
-    shards = lax.axis_size("seq")
-    my_index = lax.axis_index("seq")
-    pick_list = chosen[0, 0]
-    chosen_count = pick_list.shape[0]
-    slot_cap = tok_dev // 4
-    seq_length = tok_dev * shards
+def shard_layout(pick_list, shards, tok_dev):
     owner_of = pick_list // tok_dev
     shard_ids = jnp.arange(shards, dtype=jnp.int32)
     counts = jnp.sum((owner_of[:, None] == shard_ids[None, :]).astype(jnp.int32), axis=0)
     starts = jnp.cumsum(counts) - counts
-    padded_list = jnp.concatenate([pick_list, jnp.full((slot_cap,), seq_length, jnp.int32)])
+    return owner_of, counts, starts
+
+
+def local_slots(pick_list, shards, tok_dev, slot_cap, my_index):
+    _, counts, starts = shard_layout(pick_list, shards, tok_dev)
+    padded = jnp.concatenate([pick_list, jnp.zeros((slot_cap,), jnp.int32)])
     slot_ids = jnp.arange(slot_cap, dtype=jnp.int32)
-    my_start = starts[my_index]
-    my_count = counts[my_index]
-    my_pos = lax.dynamic_slice_in_dim(padded_list, my_start, slot_cap)
-    my_live = slot_ids < my_count
-    local_rows = jnp.where(my_live, my_pos - my_index * tok_dev, 0)
-    raw_rows = jnp.take(tokens, local_rows, axis=0)
-    raw_rows = jnp.where(my_live[:, None], raw_rows, jnp.zeros_like(raw_rows))
+    live = slot_ids < counts[my_index]
+    mine = lax.dynamic_slice_in_dim(padded, starts[my_index], slot_cap)
+    return jnp.where(live, mine - my_index * tok_dev, 0), live
+
+
+def per_device(incoming, chosen, norm_gain, router, w_query, w_key, w_value, w_out_t):
+    shards = lax.axis_size("seq")
+    batches = lax.axis_size("dp")
+    my_index = lax.axis_index("seq")
+    tok_dev = incoming.shape[2]
+    width = incoming.shape[3]
+    slot_cap = tok_dev // 4
+    part_width = w_query.shape[1]
+    head_cols = w_query.shape[2]
+    next_pick = shifted(chosen, "section", -1)[0, 0]
+    send_rows, send_live = local_slots(next_pick, shards, tok_dev, slot_cap, my_index)
+    picked_out = jnp.take(incoming[0, 0], send_rows, axis=0)
+    picked_out = jnp.where(send_live[:, None], picked_out, jnp.zeros_like(picked_out))
+    raw_rows = shifted(picked_out, "section", 1)
+    all_picks = lax.all_gather(chosen[:, 0], "dp", axis=0, tiled=True)
+    raw_rows, held_incoming = lax.optimization_barrier((raw_rows, incoming))
+    tokens = shifted(held_incoming, "section", 1)[0, 0]
+    pick_list = chosen[0, 0]
+    chosen_count = pick_list.shape[0]
+    local_rows, my_live = local_slots(pick_list, shards, tok_dev, slot_cap, my_index)
     router_gate = jax.nn.sigmoid(jnp.dot(raw_rows, router[0], preferred_element_type=jnp.float32))
     normed = rms_norm(raw_rows, norm_gain[0])
-    weights = (
-        lax.all_gather(w_query, "dp", axis=1, tiled=True),
-        lax.all_gather(w_key, "dp", axis=1, tiled=True),
-        lax.all_gather(w_value, "dp", axis=1, tiled=True),
-        lax.all_gather(w_out_t, "dp", axis=1, tiled=True),
+    by_part = normed.reshape(slot_cap, batches, part_width).transpose(1, 0, 2)
+    to_all = jnp.broadcast_to(by_part[:, None], (batches, shards, slot_cap, part_width))
+    spread = lax.all_to_all(
+        to_all.reshape(batches * shards * slot_cap, part_width),
+        ("dp", "seq"), split_axis=0, concat_axis=0, tiled=True,
     )
-    w_joint = jnp.concatenate([weights[0][0], weights[1][0], weights[2][0]], axis=1)
-    w_back = weights[3][0]
-    head_cols = w_back.shape[1]
-    slot_live = (slot_ids[None, :] < counts[:, None]).reshape(-1)
-    spread = lax.all_to_all(normed, "seq", split_axis=1, concat_axis=0, tiled=True)
-    slot_of = jnp.arange(chosen_count, dtype=jnp.int32) - jnp.take(starts, owner_of)
-    flat_of = owner_of * slot_cap + slot_of
-    compact = jnp.take(spread, flat_of, axis=0)
-    joint_proj = jnp.dot(
-        lax.all_gather(compact, "seq", axis=1, tiled=True),
-        w_joint,
-        preferred_element_type=jnp.float32,
+    owners, counts, starts = jax.vmap(lambda p: shard_layout(p, shards, tok_dev))(all_picks)
+    slot_of = jnp.arange(chosen_count, dtype=jnp.int32)[None] - jnp.take_along_axis(
+        starts, owners, axis=1
+    )
+    batch_ids = jnp.arange(batches, dtype=jnp.int32)
+    flat_of = (batch_ids[:, None] * shards + owners) * slot_cap + slot_of
+    compact = jnp.take(spread, flat_of.reshape(-1), axis=0)
+    partials = [
+        jnp.dot(compact, w[0], preferred_element_type=jnp.float32).astype(jnp.bfloat16)
+        for w in (w_query, w_key, w_value)
+    ]
+    joint_part = jnp.concatenate(partials, axis=1)
+    exchanged = lax.all_to_all(joint_part, "dp", split_axis=0, concat_axis=0, tiled=True)
+    joint_proj = jnp.sum(
+        exchanged.reshape(batches, chosen_count, 3 * head_cols).astype(jnp.float32), axis=0
     )
     all_live = jnp.ones((chosen_count,), dtype=bool)
     attended = attend_rows(joint_proj, pick_list, all_live, head_cols)
+    both = lax.all_gather(attended, "dp", axis=0, tiled=True)
     partial_out = lax.dot_general(
-        attended, w_back, (((1,), (1,)), ((), ())), preferred_element_type=jnp.float32
+        both, w_out_t[0], (((1,), (1,)), ((), ())), preferred_element_type=jnp.float32
+    ).astype(jnp.bfloat16)
+    slot_ids = jnp.arange(slot_cap, dtype=jnp.int32)
+    back_index = jnp.minimum(starts[:, :, None] + slot_ids, chosen_count - 1)
+    back_index = back_index + batch_ids[:, None, None] * chosen_count
+    slotted = jnp.take(partial_out, back_index.reshape(-1), axis=0)
+    returned = lax.all_to_all(slotted, ("dp", "seq"), split_axis=0, concat_axis=0, tiled=True)
+    returned = returned.reshape(batches, shards, slot_cap, part_width).astype(jnp.float32)
+    delta_rows = jnp.sum(returned, axis=1).transpose(1, 0, 2).reshape(slot_cap, width)
+    delta_rows = delta_rows.astype(jnp.bfloat16).astype(jnp.float32)
+    updated = (raw_rows.astype(jnp.float32) + router_gate[:, None] * delta_rows).astype(
+        jnp.bfloat16
     )
-    summed = lax.psum_scatter(
-        partial_out.astype(jnp.bfloat16), "seq", scatter_dimension=1, tiled=True
-    )
-    back_index = jnp.minimum(starts[:, None] + slot_ids[None, :], chosen_count - 1).reshape(-1)
-    slotted = jnp.take(summed, back_index, axis=0)
-    slotted = jnp.where(slot_live[:, None], slotted, jnp.zeros_like(slotted))
-    delta_rows = lax.all_to_all(slotted, "seq", split_axis=0, concat_axis=1, tiled=True)
-    updated = (
-        raw_rows.astype(jnp.float32) + router_gate[:, None] * delta_rows.astype(jnp.float32)
-    ).astype(jnp.bfloat16)
     target = jnp.where(my_live, local_rows, tok_dev)
     result = tokens.at[target].set(updated, mode="drop")
     return result[None, None]

time: 483 us -> 117 us (0.24)
  waiting for transfers between devices: 414 us -> 52.5 us
  between operations: 15.4 us -> 3.93 us
  starting transfers between devices: 11 us -> 20.9 us
  matrix products: 18.3 us -> 9.13 us
  local copies, waits for them, and re-layouts: 6.81 us -> 12.9 us
    all_gather x4 -> x0, waiting for transfers between devices: 363 us -> none  [the longest x1 106 us: per_device(): lax.all_gather(w_key, 'dp', axis=1, tiled=True)]
    all_to_all x2 -> x3, waiting for transfers between devices: 10.2 us -> 32.2 us  [the longest x1 13 us: per_device(): lax.all_to_all(to_all.reshape(batches * shards * slot_cap, part_width), (...]
    reduce_scatter x1 -> x0, waiting for transfers between devices: 21.6 us -> none  [per_device(): lax.psum_scatter(partial_out.astype(jnp.bfloat16), 'seq', scatter_dimensi...]
    dot_general x2 -> x4, matrix products: 17.6 us -> 8.39 us  [the longest x3 4.7 us: per_device(): jnp.dot(compact, w[0], preferred_element_type=jnp.float32)]
    all_to_all x2 -> x3, starting transfers between devices: 8.62 us -> 16.7 us  [the longest x1 6.75 us: per_device(): lax.all_to_all(to_all.reshape(batches * shards * slot_cap, part_width), (...]
    ppermute x1 -> x3, waiting for transfers between devices: 15.8 us -> 20.4 us  [shifted(): return lax.ppermute(value, axis, pairs)]
  transfers between devices with their start and end apart: 8 -> 6, of which waited for: 8 -> 5; matrix products, arithmetic and copies ran while one was open for 5% -> 6% of each run, Pallas kernels for 0% -> 0%
where the time goes in v1:
time: 117 us; the launch traced here: 115 us
  waiting for transfers between devices  52.5 us (45%)
  starting transfers between devices  20.9 us (18%)
  local copies, waits for them, and re-layouts  12.9 us (11%)
  matrix products  9.13 us (8%)
  other arithmetic  8.37 us (7%)
  blocking collectives  7.69 us (7%)
  between operations  3.93 us (3%)
    ppermute x3, waiting for transfers between devices, shifted(): return lax.ppermute(value, axis, pairs)  20.4 us
    all_to_all x1, waiting for transfers between devices, per_device(): lax.all_to_all(to_all.reshape(batches * shards * slot_cap, part_width), (...  13 us
    all_to_all x1, waiting for transfers between devices, per_device(): lax.all_to_all(joint_part, 'dp', split_axis=0, concat_axis=0, tiled=True)  9.72 us
    all_to_all x1, waiting for transfers between devices, per_device(): lax.all_to_all(slotted, ('dp', 'seq'), split_axis=0, concat_axis=0, tiled...  9.42 us
    all_to_all x1, starting transfers between devices, per_device(): lax.all_to_all(to_all.reshape(batches * shards * slot_cap, part_width), (...  6.75 us
    all_to_all x1, starting transfers between devices, per_device(): lax.all_to_all(slotted, ('dp', 'seq'), split_axis=0, concat_axis=0, tiled...  6.38 us
    dot_general x3, matrix products, per_device(): jnp.dot(compact, w[0], preferred_element_type=jnp.float32)  4.7 us
    all_gather x1, blocking collectives, per_device(): both = lax.all_gather(attended, 'dp', axis=0, tiled=True)  4.5 us
  transfers between devices with their start and end apart: 6, of which 5 were waited for; matrix products, arithmetic and copies ran while one was open for 6% of the time, Pallas kernels for 0%

profile of v1, /device:TPU:1, one launch (start us, length us, event | category | flops | bytes accessed | tf_op | source)
XLA Modules:
  0.0 115.4 jit_solution(2274883813332386113)
XLA Ops:
  0.0 4.2 %collective-permute-start = (s32[1,1,64]{2,1,0:T(1,128)}, s32[1,1,64]{2,1,0:T(1,128)S(1)}, u32[]{:S(2)}, u32[]{:S(2)}) collective-permute-start(s32[1,1,64]{2,1,0:T(1,128)} %param.9), channel_id=1, source_target_pairs={{0,24},{8,0},{16,8},{24,16},{1,25},{9,1},{17,9},{25,17},{2,26},{10... | collective-permute-start | bytes 776 | tf_op jit(solution)/shard_map/ppermute | solution.py:17
  4.2 0.7 bitcast_convert_fusion
  4.9 3.2 %all-gather = s32[2,1,64]{2,1,0:T(1,128)S(1)} all-gather(s32[1,1,64]{2,1,0:T(1,128)} %param.9), channel_id=2, replica_groups=mesh['section'=4,'dp'=2,'seq'=4] {'dp'}, dimensions={0}, use_global_device_ids=true | all-gather | bytes 768 | tf_op jit(solution)/shard_map/all_gather | solution.py:99
  8.1 0.1 convert_reduce_fusion.1
  8.3 0.2 reduce_window_sum.20
  8.5 1.5 %gather_fusion.3 = s32[128]{0:T(128)S(1)} fusion(s32[2,4]{1,0:T(2,128)S(1)} %sub.73, s32[128]{0:T(128)S(1)} %reshape.427), kind=kCustom, calls=%fused_computation.3 | custom fusion | bytes 2048 | tf_op jit(solution)/shard_map/jit(take_along_axis)/gather | solution.py:114
  10.4 0.7 dynamic_slice.18
  11.1 0.2 reduce-window.18
  11.3 0.6 dynamic_slice.19
  13.8 0.8 compare_and_fusion.1
  14.6 2.3 %gather_fusion = bf16[32,4096]{1,0:T(8,128)(2,1)S(1)} fusion(bf16[128,4096]{1,0:T(8,128)(2,1)} %bitcast.94, s32[1024]{0:T(1024)S(1)} %pad_clamp_fusion.2), kind=kCustom, calls=%fused_computation | custom fusion | bytes 524416 | tf_op jit(solution)/shard_map/jit(_take)/gather | solution.py:96
  17.1 7.4 %collective-permute-done.1 = bf16[32,4096]{1,0:T(8,128)(2,1)S(1)} collective-permute-done((bf16[32,4096]{1,0:T(8,128)(2,1)S(1)}, bf16[32,4096]{1,0:T(8,128)(2,1)S(1)}, u32[]{:S(2)}, u32[]{:S(2)}) %collective-permute-start.1) | collective-permute-done | bytes 262176 | tf_op jit(solution)/shard_map/ppermute | solution.py:17
  24.5 0.2 fusion.29
  24.7 0.1 fusion.31
  24.9 0.2 reshape.396
  25.1 1.1 broadcast_in_dim.109
  26.2 6.7 %all-to-all-start = ((bf16[8,32,2048]{2,1,0:T(8,128)(2,1)}), bf16[8,32,2048]{2,1,0:T(8,128)(2,1)S(1)}, u32[]{:S(2)}, u32[]{:S(2)}) async-start(bf16[8,32,2048]{2,1,0:T(8,128)(2,1)} %bitcast.17), calls=%async_computation | async-start | bytes 2097152 | tf_op jit(solution)/shard_map/all_to_all | solution.py:109
  33.6 13.0 %all-to-all-done = bf16[8,32,2048]{2,1,0:T(8,128)(2,1)S(1)} async-done(((bf16[8,32,2048]{2,1,0:T(8,128)(2,1)}), bf16[8,32,2048]{2,1,0:T(8,128)(2,1)S(1)}, u32[]{:S(2)}, u32[]{:S(2)}) %all-to-all-start) | async-done | bytes 1048608 | tf_op jit(solution)/shard_map/all_to_all | solution.py:109
  46.6 0.9 gather_fusion.1
  47.5 3.1 %fusion.16 = bf16[128,1024]{1,0:T(8,128)(2,1)S(1)} fusion(bf16[1,2048,1024]{2,1,0:T(8,128)(2,1)} %param.13, bf16[128,2048]{1,0:T(8,128)(2,1)S(1)} %gather_fusion.1, pred[128]{0:T(512)(128)(4,1)S(1)} %compare_and_fusion), kind=kOutput, calls=%fused_computation.18 | convolution fusion | flops 537264128 | bytes 4980864 | tf_op jit(solution)/shard_map/dot_general | solution.py:121
  50.7 0.3 copy-done.1
  51.0 0.8 fusion.19
  51.8 0.5 copy-done.2
  52.2 0.8 fusion.13
  53.0 0.9 pad_maximum_fusion
  54.0 3.5 %all-to-all-start.1 = ((bf16[2,64,3072]{2,1,0:T(8,128)(2,1)}), bf16[2,64,3072]{2,1,0:T(8,128)(2,1)S(1)}, u32[]{:S(2)}, u32[]{:S(2)}) async-start(bf16[2,64,3072]{2,1,0:T(8,128)(2,1)} %bitcast.23), calls=%async_computation.1 | async-start | bytes 1572864 | tf_op jit(solution)/shard_map/all_to_all | solution.py:125
  57.6 0.2 multiply_cosine_fusion
  57.8 9.7 %all-to-all-done.1 = bf16[2,64,3072]{2,1,0:T(8,128)(2,1)S(1)} async-done(((bf16[2,64,3072]{2,1,0:T(8,128)(2,1)}), bf16[2,64,3072]{2,1,0:T(8,128)(2,1)S(1)}, u32[]{:S(2)}, u32[]{:S(2)}) %all-to-all-start.1) | async-done | bytes 786464 | tf_op jit(solution)/shard_map/all_to_all | solution.py:125
  67.8 0.1 fusion.68
  67.9 0.1 fusion.67
  68.1 0.2 subtract_convert_fusion
  68.3 0.3 fusion.69
  68.6 0.2 fusion.24
  68.9 4.5 %all_gather.7 = bf16[128,1024]{1,0:T(8,128)(2,1)S(1)} all-gather(bf16[64,1024]{1,0:T(8,128)(2,1)S(1)} %bitcast.102), channel_id=1, replica_groups=mesh['section'=4,'dp'=2,'seq'=4] {'dp'}, dimensions={0}, use_global_device_ids=true | all-gather | bytes 393216 | tf_op jit(solution)/shard_map/all_gather | solution.py:131
  73.4 3.7 %fusion.9 = bf16[128,2048]{1,0:T(8,128)(2,1)S(1)} fusion(bf16[128,1024]{1,0:T(8,128)(2,1)S(1)} %all_gather.7, bf16[1,2048,1024]{2,1,0:T(8,128)(2,1)} %param.15), kind=kOutput, calls=%fused_computation.14 | convolution fusion | flops 537133056 | bytes 4980736 | tf_op jit(solution)/shard_map/dot_general | solution.py:132
  77.1 1.4 %gather_fusion.2 = bf16[256,2048]{1,0:T(8,128)(2,1)S(1)} fusion(bf16[128,2048]{1,0:T(8,128)(2,1)S(1)} %fusion.9, s32[1024]{0:T(1024)S(1)} %pad_clamp_fusion), kind=kCustom, calls=%fused_computation.2 | custom fusion | bytes 2098176 | tf_op jit(solution)/shard_map/jit(_take)/gather | solution.py:138
  78.5 1.1 broadcast_select_fusion
  79.6 6.4 %all-to-all-start.2 = ((bf16[8,32,2048]{2,1,0:T(8,128)(2,1)}), bf16[8,32,2048]{2,1,0:T(8,128)(2,1)S(1)}, u32[]{:S(2)}, u32[]{:S(2)}) async-start(bf16[8,32,2048]{2,1,0:T(8,128)(2,1)} %broadcast_select_fusion), calls=%async_computation.2 | async-start | bytes 2097152 | tf_op jit(solution)/shard_map/all_to_all | solution.py:139
  86.1 0.2 reduce-window.19
  86.3 0.7 dynamic_slice.21
  87.0 0.6 dynamic_slice.22
  89.2 0.8 compare_select_fusion.5
  90.0 0.2 fusion.28
  90.2 9.4 %all-to-all-done.2 = bf16[8,32,2048]{2,1,0:T(8,128)(2,1)S(1)} async-done(((bf16[8,32,2048]{2,1,0:T(8,128)(2,1)}), bf16[8,32,2048]{2,1,0:T(8,128)(2,1)S(1)}, u32[]{:S(2)}, u32[]{:S(2)}) %all-to-all-start.2) | async-done | bytes 1048608 | tf_op jit(solution)/shard_map/all_to_all | solution.py:139
  99.6 0.1 bitcast_reduce_fusion
  99.8 13.0 %collective-permute-done.2 = bf16[1,1,128,4096]{3,2,1,0:T(8,128)(2,1)S(1)} collective-permute-done((bf16[1,1,128,4096]{3,2,1,0:T(8,128)(2,1)S(1)}, bf16[1,1,128,4096]{3,2,1,0:T(8,128)(2,1)S(1)}, u32[]{:S(2)}, u32[]{:S(2)}) %collective-permute-start.2) | collective-permute-done | bytes 1048608 | tf_op jit(solution)/shard_map/ppermute | solution.py:17
  112.8 1.6 %scatter_custom_fusion = bf16[128,4096]{1,0:T(8,128)(2,1)S(1)} fusion(bf16[128,4096]{1,0:T(8,128)(2,1)S(1)} %bitcast.99, s32[32]{0:T(128)S(1)} %compare_select_fusion.5, bf16[32,4096]{1,0:T(8,128)(2,1)S(1)} %collective-permute-done.1, f32[32,4096]{1,0:T(8,128)S(1)} %bitcast.98, f32[32]{0:T(128)S(1)} %fusion.28), kind=kCustom, calls=%fused_computation.42 | custom fusion | flops 524288 | bytes 1835520 | tf_op jit(solution)/shard_map/scatter | solution.py:147
  114.5 1.0 copy.63
  (52 shorter events, 1.9 us)
Async XLA Ops:
  0.0 90.0 %copy-start = (bf16[1,4096]{1,0:T(2,128)(2,1)S(1)}, bf16[1,4096]{1,0:T(2,128)(2,1)}, u32[]{:S(2)}) copy-start(bf16[1,4096]{1,0:T(2,128)(2,1)} %param.11) | copy-start | bytes 24580
  0.0 24.7 %copy-start.4 = (f32[1,4096]{1,0:T(1,128)S(1)}, f32[1,4096]{1,0:T(1,128)}, u32[]{:S(2)}) copy-start(f32[1,4096]{1,0:T(1,128)} %param.10) | copy-start | bytes 49156
  0.0 10.3 %collective-permute-start = (s32[1,1,64]{2,1,0:T(1,128)}, s32[1,1,64]{2,1,0:T(1,128)S(1)}, u32[]{:S(2)}, u32[]{:S(2)}) collective-permute-start(s32[1,1,64]{2,1,0:T(1,128)} %param.9), channel_id=1, source_target_pairs={{0,24},{8,0},{16,8},{24,16},{1,25},{9,1},{17,9},{25,17},{2,26},{10... | collective-permute-start | bytes 776 | tf_op jit(solution)/shard_map/ppermute | solution.py:17
  10.0 23.5 %copy-start.5 = (s32[1,1,64]{2,1,0:T(1,128)S(1)}, s32[1,1,64]{2,1,0:T(1,128)}, u32[]{:S(2)}) copy-start(s32[1,1,64]{2,1,0:T(1,128)} %param.9) | copy-start | bytes 772
  17.0 7.5 %collective-permute-start.1 = (bf16[32,4096]{1,0:T(8,128)(2,1)S(1)}, bf16[32,4096]{1,0:T(8,128)(2,1)S(1)}, u32[]{:S(2)}, u32[]{:S(2)}) collective-permute-start(bf16[32,4096]{1,0:T(8,128)(2,1)S(1)} %select_select_fusion), channel_id=1, source_target_pairs={{0,8},{8,16},{16,24},{24,0},{1,9},{9,17},{17,25},{25,1},{2,10},{10... | collective-permute-start | bytes 786440 | tf_op jit(solution)/shard_map/ppermute | solution.py:17
  26.2 20.3 %all-to-all-start = ((bf16[8,32,2048]{2,1,0:T(8,128)(2,1)}), bf16[8,32,2048]{2,1,0:T(8,128)(2,1)S(1)}, u32[]{:S(2)}, u32[]{:S(2)}) async-start(bf16[8,32,2048]{2,1,0:T(8,128)(2,1)} %bitcast.17), calls=%async_computation | async-start | bytes 2097152 | tf_op jit(solution)/shard_map/all_to_all | solution.py:109
  47.5 3.5 %copy-start.1 = (bf16[1,2048,1024]{2,1,0:T(8,128)(2,1)S(1)}, bf16[1,2048,1024]{2,1,0:T(8,128)(2,1)}, u32[]{:S(2)}) copy-start(bf16[1,2048,1024]{2,1,0:T(8,128)(2,1)} %param.14) | copy-start | bytes 12582916
  47.5 4.7 %copy-start.2 = (bf16[1,2048,1024]{2,1,0:T(8,128)(2,1)S(1)}, bf16[1,2048,1024]{2,1,0:T(8,128)(2,1)}, u32[]{:S(2)}) copy-start(bf16[1,2048,1024]{2,1,0:T(8,128)(2,1)} %param.12) | copy-start | bytes 12582916
  54.0 13.5 %all-to-all-start.1 = ((bf16[2,64,3072]{2,1,0:T(8,128)(2,1)}), bf16[2,64,3072]{2,1,0:T(8,128)(2,1)S(1)}, u32[]{:S(2)}, u32[]{:S(2)}) async-start(bf16[2,64,3072]{2,1,0:T(8,128)(2,1)} %bitcast.23), calls=%async_computation.1 | async-start | bytes 1572864 | tf_op jit(solution)/shard_map/all_to_all | solution.py:125
  78.4 7.8 %copy-start.3 = (bf16[1,1,128,4096]{3,2,1,0:T(8,128)(2,1)S(1)}, bf16[1,1,128,4096]{3,2,1,0:T(8,128)(2,1)}, u32[]{:S(2)}) copy-start(bf16[1,1,128,4096]{3,2,1,0:T(8,128)(2,1)} %param.8) | copy-start | bytes 3145732
  79.6 20.0 %all-to-all-start.2 = ((bf16[8,32,2048]{2,1,0:T(8,128)(2,1)}), bf16[8,32,2048]{2,1,0:T(8,128)(2,1)S(1)}, u32[]{:S(2)}, u32[]{:S(2)}) async-start(bf16[8,32,2048]{2,1,0:T(8,128)(2,1)} %broadcast_select_fusion), calls=%async_computation.2 | async-start | bytes 2097152 | tf_op jit(solution)/shard_map/all_to_all | solution.py:139
  86.3 26.5 %collective-permute-start.2 = (bf16[1,1,128,4096]{3,2,1,0:T(8,128)(2,1)S(1)}, bf16[1,1,128,4096]{3,2,1,0:T(8,128)(2,1)S(1)}, u32[]{:S(2)}, u32[]{:S(2)}) collective-permute-start(bf16[1,1,128,4096]{3,2,1,0:T(8,128)(2,1)S(1)} %copy-done.3), channel_id=1, source_target_pairs={{0,8},{8,16},{16,24},{24,0},{1,9},{9,17},{17,25},{25,1},{2,10},{10... | collective-permute-start | bytes 3145736 | tf_op jit(solution)/shard_map/ppermute | solution.py:17

commit v2 on v0

v2 whole, which is shorter than its diff:
```python
import functools

import jax
import jax.numpy as jnp
import numpy as np
from jax import lax
from jax.experimental import pallas as pl
from jax.experimental.pallas import tpu as pltpu
from jax.sharding import PartitionSpec as P

HD = 128


EPSILON = 1e-05
ROPE_BASE = 500000.0
NEG_FILL = -1e30
MESH = pl.DeviceIdType.MESH
F32 = jnp.float32
BF16 = jnp.bfloat16


def nt_dot(lhs, rhs):
    return lax.dot_general(lhs, rhs, (((1,), (1,)), ((), ())), preferred_element_type=F32)


def nn_dot(lhs, rhs):
    return jnp.dot(lhs, rhs, preferred_element_type=F32)


def ones_where(mask):
    return jnp.where(mask, 1.0, 0.0).astype(BF16)


def iota_f32(shape, dim):
    return lax.broadcasted_iota(jnp.int32, shape, dim).astype(F32)


def as_column(row):
    count = row.shape[1]
    eye = lax.broadcasted_iota(jnp.int32, (count, count), 0) == lax.broadcasted_iota(
        jnp.int32, (count, count), 1
    )
    return jnp.sum(jnp.where(eye, row, 0.0), axis=1, keepdims=True)


def count_below(picks, bound):
    return jnp.sum(jnp.where(picks < bound, 1.0, 0.0), axis=1, keepdims=True)


def local_onehots(picks, lowest, slots, tok_dev):
    count = picks.shape[1]
    mine = (picks >= lowest) & (picks < lowest + tok_dev)
    slot = iota_f32((1, count), 1) - count_below(picks, lowest)
    slot = jnp.where(mine, slot, -1.0)
    by_slot = ones_where(slot == iota_f32((slots, count), 0))
    by_row = ones_where((picks - lowest).astype(F32) == iota_f32((tok_dev, count), 0))
    return by_slot, by_row


def flat_slots(picks, shards, slots, tok_dev):
    count = picks.shape[1]
    order = iota_f32((1, count), 1)
    flat = jnp.zeros((1, count), F32)
    for owner in range(shards):
        low = owner * tok_dev
        inside = (picks >= low) & (picks < low + tok_dev)
        flat = jnp.where(inside, owner * slots + order - count_below(picks, low), flat)
    return flat


def kernel(
    sections, batches, shards,
    tokens, chosen, gain, router, freq, w_q, w_k, w_v, w_o,
    out,
    w_in, w_back, picks, next_pick, picked, raw_rows, arrived, normed, spread,
    compact, part, joint, attended, both, slot_att, out_part, returned,
    w_sem, pick_send, pick_recv, row_send, row_recv, sp_send, sp_recv,
    jt_send, jt_recv, at_send, at_recv, rt_send, rt_recv,
):
    z, g, t = lax.axis_index("section"), lax.axis_index("dp"), lax.axis_index("seq")
    plane = batches * shards
    me = g * shards + t
    after = (lax.rem(z + 1, sections), g, t)
    before = (lax.rem(z + sections - 1, sections), g, t)
    tok_dev, width = tokens.shape
    count = chosen.shape[1]
    slots = tok_dev // 4
    depth, head_cols = w_q.shape

    loads = [
        pltpu.make_async_copy(w, w_in.at[i], w_sem.at[i]) for i, w in enumerate((w_q, w_k, w_v))
    ]
    loads.append(pltpu.make_async_copy(w_o, w_back, w_sem.at[3]))
    for load in loads:
        load.start()

    def peer(step):
        index = lax.rem(me + step, plane)
        return index, (z, lax.div(index, shards), lax.rem(index, shards))

    def mate(step):
        index = lax.rem(g + step, batches)
        return index, (z, index, t)

    def remote(src, dst, send, recv, device):
        return pltpu.make_async_remote_copy(
            src_ref=src, dst_ref=dst, send_sem=send, recv_sem=recv,
            device_id=device, device_id_type=MESH,
        )

    barrier = pltpu.get_barrier_semaphore()
    for device in (after, before):
        pl.semaphore_signal(barrier, inc=1, device_id=device, device_id_type=MESH)

    @pl.loop(1, plane)
    def _(step):
        pl.semaphore_signal(barrier, inc=1, device_id=peer(step)[1], device_id_type=MESH)

    my_picks = chosen[...]
    pick_cols = picks.shape[2]
    padded = my_picks
    if pick_cols > count:
        padded = jnp.concatenate(
            [my_picks, jnp.zeros((1, pick_cols - count), jnp.int32)], axis=1
        )
    picks[g] = jnp.broadcast_to(padded, (8, pick_cols))
    pl.semaphore_wait(barrier, plane + 1)

    pick_back = remote(
        picks.at[g], next_pick, pick_send.at[0], pick_recv.at[batches], before
    )
    pick_back.start()

    def pick_copy(step):
        index, device = mate(step)
        return remote(picks.at[g], picks.at[g], pick_send.at[step], pick_recv.at[g], device)

    for step in range(1, batches):
        pick_copy(step).start()

    pick_back.wait_recv()
    lowest = t * tok_dev
    by_slot, by_row = local_onehots(next_pick[0:1, :count], lowest, slots, tok_dev)
    gather = nt_dot(by_slot, by_row).astype(BF16)
    picked[...] = nn_dot(gather, tokens[...]).astype(BF16)
    row_copy = remote(picked, raw_rows, row_send.at[0], row_recv.at[0], after)
    row_copy.start()

    angles = as_column(my_picks.astype(F32)) * freq[...]
    cosine = jnp.cos(angles)
    lane = lax.broadcasted_iota(jnp.int32, (count, HD), 1)
    sine = jnp.where(lane < HD // 2, -1.0, 1.0) * jnp.sin(angles)

    row_copy.wait_recv()
    relay = remote(tokens, arrived, row_send.at[1], row_recv.at[1], after)
    relay.start()
    rows = raw_rows[...].astype(F32)
    inv_scale = lax.rsqrt(jnp.mean(rows * rows, axis=1, keepdims=True) + EPSILON)
    scaled = (rows * inv_scale * gain[...]).astype(BF16)
    for b in range(batches):
        normed[b] = scaled[:, b * depth : (b + 1) * depth]

    def spread_copy(step):
        index, device = peer(step)
        return remote(
            normed.at[lax.div(index, shards)], spread.at[me],
            sp_send.at[index], sp_recv.at[me], device,
        )

    @pl.loop(1, plane)
    def _(step):
        spread_copy(step).start()

    spread[me] = normed[g]
    gate = jax.nn.sigmoid(
        jnp.sum(rows * router[...].astype(F32), axis=1, keepdims=True)
    )

    def arrived_from(buffer, sems, index):
        remote(buffer.at[index], buffer.at[index], sems.at[index], sems.at[index], after).wait_recv()

    for step in range(1, batches):
        arrived_from(picks, pick_recv, mate(step)[0])
    flats = [flat_slots(picks[b, 0:1, :count], shards, slots, tok_dev) for b in range(batches)]
    flat_cols = [as_column(flat) for flat in flats]

    @pl.loop(1, plane)
    def _(step):
        arrived_from(spread, sp_recv, peer(step)[0])

    for b in range(batches):
        choose = ones_where(flat_cols[b] == iota_f32((count, shards * slots), 1))
        source = spread[b * shards : (b + 1) * shards].reshape(shards * slots, depth)
        compact[b * count : (b + 1) * count, :] = nn_dot(choose, source).astype(BF16)

    cols = min(256, head_cols)

    def joint_copy(step, which):
        index, device = mate(step)
        return remote(
            part.at[index, which], joint.at[g, which],
            jt_send.at[step, which], jt_recv.at[g, which], device,
        )

    for which in range(3):
        loads[which].wait()

        @pl.loop(0, head_cols // cols)
        def _(block):
            at = pl.ds(pl.multiple_of(block * cols, cols), cols)
            product = nn_dot(compact[...], w_in[which, :, at]).astype(BF16)
            for b in range(batches):
                part[b, which, :, at] = product[b * count : (b + 1) * count]

        for step in range(1, batches):
            joint_copy(step, which).start()
        joint[g, which] = part[g, which]

    summed = []
    for which in range(3):
        for step in range(1, batches):
            index = mate(step)[0]
            slot = joint.at[index, which]
            remote(
                slot, slot, jt_recv.at[index, which], jt_recv.at[index, which], after
            ).wait_recv()
        total = joint[0, which].astype(F32)
        for b in range(1, batches):
            total = total + joint[b, which].astype(F32)
        summed.append(total)

    def rope(value):
        swapped = jnp.concatenate([value[:, HD // 2 :], value[:, : HD // 2]], axis=1)
        return (value * cosine + swapped * sine).astype(BF16)

    causal = lax.broadcasted_iota(jnp.int32, (count, count), 1) <= lax.broadcasted_iota(
        jnp.int32, (count, count), 0
    )
    for head in range(head_cols // HD):
        at = slice(head * HD, (head + 1) * HD)
        scores = nt_dot(rope(summed[0][:, at]), rope(summed[1][:, at])) * HD ** (-0.5)
        scores = jnp.where(causal, scores, NEG_FILL)
        exponent = jnp.exp(scores - jnp.max(scores, axis=1, keepdims=True))
        weights = (exponent / jnp.sum(exponent, axis=1, keepdims=True)).astype(BF16)
        attended[:, at] = nn_dot(weights, summed[2][:, at].astype(BF16)).astype(BF16)

    def attended_copy(step):
        index, device = mate(step)
        return remote(attended, both.at[g], at_send.at[step], at_recv.at[g], device)

    for step in range(1, batches):
        attended_copy(step).start()
    both[g] = attended[...]
    loads[3].wait()

    def return_copy(index):
        device = (z, lax.div(index, shards), lax.rem(index, shards))
        return remote(
            out_part.at[index], returned.at[me], rt_send.at[index], rt_recv.at[me], device
        )

    out_cols = min(256, depth)
    for step in range(batches):
        batch = mate(step)[0]
        if step:
            arrived_from(both, at_recv, batch)
        place = flat_slots(picks[batch, 0:1, :count], shards, slots, tok_dev)
        place = ones_where(place == iota_f32((shards * slots, count), 0))
        slot_att[...] = nn_dot(place, both[batch]).astype(BF16)

        @pl.loop(0, depth // out_cols)
        def _(block):
            start = pl.multiple_of(block * out_cols, out_cols)
            at = pl.ds(start, out_cols)
            product = nt_dot(slot_att[...], w_back[at, :]).astype(BF16)
            for owner in range(shards):
                out_part[batch * shards + owner, :, at] = product[
                    owner * slots : (owner + 1) * slots
                ]

        @pl.loop(1 if step == 0 else 0, shards)
        def _(turn):
            return_copy(batch * shards + lax.rem(t + turn, shards)).start()

    returned[me] = out_part[me]
    by_slot, by_row = local_onehots(my_picks, lowest, slots, tok_dev)
    scatter = nt_dot(by_row, by_slot).astype(BF16)
    held = jnp.sum(by_row.astype(F32), axis=1, keepdims=True) > 0.5
    relay.wait_recv()

    @pl.loop(1, plane)
    def _(step):
        arrived_from(returned, rt_recv, peer(step)[0])

    for b in range(batches):
        at = slice(b * depth, (b + 1) * depth)
        delta = returned[b * shards].astype(F32)
        for owner in range(1, shards):
            delta = delta + returned[b * shards + owner].astype(F32)
        delta = delta.astype(BF16).astype(F32)
        updated = (raw_rows[:, at].astype(F32) + gate * delta).astype(BF16)
        replaced = nn_dot(scatter, updated)
        out[:, at] = jnp.where(held, replaced, arrived[:, at].astype(F32)).astype(BF16)

    pick_back.wait_send()
    row_copy.wait_send()
    relay.wait_send()
    for step in range(1, batches):
        pick_copy(step).wait_send()
        attended_copy(step).wait_send()
        for which in range(3):
            joint_copy(step, which).wait_send()

    @pl.loop(1, plane)
    def _(step):
        spread_copy(step).wait_send()
        return_copy(peer(step)[0]).wait_send()


def per_device(incoming, chosen, norm_gain, router, w_query, w_key, w_value, w_out_t):
    sections = lax.axis_size("section")
    batches = lax.axis_size("dp")
    shards = lax.axis_size("seq")
    plane = batches * shards
    tok_dev, width = incoming.shape[2:]
    count = chosen.shape[2]
    slots = tok_dev // 4
    depth, head_cols = w_query.shape[1:]
    half = np.arange(HD // 2, dtype=np.float32)
    freq = np.float32(ROPE_BASE) ** (np.float32(-2.0) * half / np.float32(HD))
    freq = jnp.asarray(np.concatenate([freq, freq])[None].astype(np.float32))
    pick_cols = -(-count // 128) * 128
    vmem = pl.BlockSpec(memory_space=pltpu.VMEM)
    hbm = pl.BlockSpec(memory_space=pl.ANY)
    dma = pltpu.SemaphoreType.DMA
    result = pl.pallas_call(
        functools.partial(kernel, sections, batches, shards),
        out_shape=jax.ShapeDtypeStruct((tok_dev, width), BF16),
        in_specs=[vmem] * 5 + [hbm] * 4,
        out_specs=vmem,
        scratch_shapes=[
            pltpu.VMEM((3, depth, head_cols), BF16),
            pltpu.VMEM((depth, head_cols), BF16),
            pltpu.VMEM((batches, 8, pick_cols), jnp.int32),
            pltpu.VMEM((8, pick_cols), jnp.int32),
            pltpu.VMEM((slots, width), BF16),
            pltpu.VMEM((slots, width), BF16),
            pltpu.VMEM((tok_dev, width), BF16),
            pltpu.VMEM((batches, slots, depth), BF16),
            pltpu.VMEM((plane, slots, depth), BF16),
            pltpu.VMEM((batches * count, depth), BF16),
            pltpu.VMEM((batches, 3, count, head_cols), BF16),
            pltpu.VMEM((batches, 3, count, head_cols), BF16),
            pltpu.VMEM((count, head_cols), BF16),
            pltpu.VMEM((batches, count, head_cols), BF16),
            pltpu.VMEM((shards * slots, head_cols), BF16),
            pltpu.VMEM((plane, slots, depth), BF16),
            pltpu.VMEM((plane, slots, depth), BF16),
            dma((4,)),
            dma((batches,)), dma((batches + 1,)),
            dma((2,)), dma((2,)),
            dma((plane,)), dma((plane,)),
            dma((batches, 3)), dma((batches, 3)),
            dma((batches,)), dma((batches,)),
            dma((plane,)), dma((plane,)),
        ],
        compiler_params=pltpu.CompilerParams(
            collective_id=0, has_side_effects=True, vmem_limit_bytes=52 * 1024 * 1024
        ),
    )(
        incoming[0, 0], chosen[0], norm_gain, router, freq,
        w_query[0], w_key[0], w_value[0], w_out_t[0],
    )
    return result[None, None]


def solution(mesh):
    in_specs = (
        P("section", "dp", "seq", None),
        P("section", "dp", None),
        P("section", None),
        P("section", None),
        P("section", "dp", "seq"),
        P("section", "dp", "seq"),
        P("section", "dp", "seq"),
        P("section", "dp", "seq"),
    )
    out_specs = P("section", "dp", "seq", None)
    return jax.shard_map(
        per_device, mesh=mesh, in_specs=in_specs, out_specs=out_specs, check_vma=False
    )
```

time: 483 us -> 68.7 us (0.14)
  waiting for transfers between devices: 414 us -> 0 us
  Pallas kernels: 0 us -> 64.6 us
  matrix products: 18.3 us -> 0 us
  between operations: 15.4 us -> 0.01 us
  starting transfers between devices: 11 us -> 0 us
  other arithmetic: 9.33 us -> 0 us
  blocking collectives: 7.29 us -> 0 us
    all_gather x4 -> x0, waiting for transfers between devices: 363 us -> none  [the longest x1 106 us: per_device(): lax.all_gather(w_key, 'dp', axis=1, tiled=True)]
    pallas_call x0 -> x1, Pallas kernels: none -> 64.6 us  [per_device(): pl.pallas_call(functools.partial(kernel, sections, batches, shards), out_...]
    reduce_scatter x1 -> x0, waiting for transfers between devices: 21.6 us -> none  [per_device(): lax.psum_scatter(partial_out.astype(jnp.bfloat16), 'seq', scatter_dimensi...]
    dot_general x4 -> x0, matrix products: 18 us -> none  [the longest x1 10.7 us: per_device(): jnp.dot(lax.all_gather(compact, 'seq', axis=1, tiled=True), w_joint, pref...]
    ppermute x1 -> x0, waiting for transfers between devices: 15.8 us -> none  [shifted(): return lax.ppermute(value, axis, pairs)]
    all_to_all x2 -> x0, waiting for transfers between devices: 10.2 us -> none  [the longest x1 5.2 us: per_device(): lax.all_to_all(normed, 'seq', split_axis=1, concat_axis=0, tiled=True)]
    all_to_all x2 -> x0, starting transfers between devices: 8.62 us -> none  [the longest x1 4.6 us: per_device(): lax.all_to_all(normed, 'seq', split_axis=1, concat_axis=0, tiled=True)]
    all_gather x1 -> x0, blocking collectives: 7.29 us -> none  [per_device(): lax.all_gather(compact, 'seq', axis=1, tiled=True)]
  transfers between devices with their start and end apart: 8 -> 0, of which waited for: 8 -> 0; matrix products, arithmetic and copies ran while one was open for 5% -> 0% of each run, Pallas kernels for 0% -> 0%
where the time goes in v2:
time: 68.7 us; the launch traced here: 68.3 us
  Pallas kernels  64.6 us (94%)
  local copies, waits for them, and re-layouts  3.72 us (5%)
    pallas_call x1, Pallas kernels, per_device(): pl.pallas_call(functools.partial(kernel, sections, batches, shards), out_...  64.6 us
    unnamed x9, local copies, waits for them, and re-layouts  3.72 us

profile of v2, /device:TPU:1, one launch (start us, length us, event | category | flops | bytes accessed | tf_op | source)
XLA Modules:
  0.0 68.3 jit_solution(14669316189056428740)
XLA Ops:
  0.0 0.0 copy-start
  0.0 0.7 %copy-done = f32[1,4096]{1,0:T(1,128)S(1)} copy-done((f32[1,4096]{1,0:T(1,128)S(1)}, f32[1,4096]{1,0:T(1,128)}, u32[]{:S(2)}) %copy-start) | copy-done | bytes 16408
  0.7 0.0 copy-start.1
  0.7 0.7 %copy-done.1 = bf16[1,4096]{1,0:T(2,128)(2,1)S(1)} copy-done((bf16[1,4096]{1,0:T(2,128)(2,1)S(1)}, bf16[1,4096]{1,0:T(2,128)(2,1)}, u32[]{:S(2)}) %copy-start.1) | copy-done | bytes 8216
  1.4 0.0 copy-start.2
  1.4 0.7 copy-done.2
  2.1 0.0 copy-start.3
  2.1 0.7 copy-done.3
  2.7 64.6 %shard_map.91 = bf16[128,4096]{1,0:T(8,128)(2,1)S(1)} custom-call(bf16[128,4096]{1,0:T(8,128)(2,1)} %bitcast.13, s32[1,64]{1,0:T(1,128)S(1)} %bitcast.8, f32[1,4096]{1,0:T(1,128)S(1)} %copy-done, bf16[1,4096]{1,0:T(2,128)(2,1)S(1)} %copy-done.1, f32[1,128]{1,0:T(1,128)S(1)} %copy-done.3, bf16[2048,1024]{1,0:T(8,128)(2,1)} %bitcast.9, ...), custom_call_target="tpu_custom_call" | custom-call | tf_op jit(solution)/shard_map/pallas_call | solution.py:336
  67.4 1.0 %copy.11 = bf16[1,1,128,4096]{3,2,1,0:T(8,128)(2,1)} copy(bf16[1,1,128,4096]{3,2,1,0:T(8,128)(2,1)S(1)} %bitcast.7) | data formatting | bytes 2097152
Async XLA Ops:
  0.0 0.7 %copy-start = (f32[1,4096]{1,0:T(1,128)S(1)}, f32[1,4096]{1,0:T(1,128)}, u32[]{:S(2)}) copy-start(f32[1,4096]{1,0:T(1,128)} %gain.1) | copy-start | bytes 49156
  0.7 0.7 %copy-start.1 = (bf16[1,4096]{1,0:T(2,128)(2,1)S(1)}, bf16[1,4096]{1,0:T(2,128)(2,1)}, u32[]{:S(2)}) copy-start(bf16[1,4096]{1,0:T(2,128)(2,1)} %router.1) | copy-start | bytes 24580
  1.4 0.7 copy-start.2
  2.1 0.7 copy-start.3

commit v3 on v2

--- a/solution.py
+++ b/solution.py
@@ -70,16 +70,20 @@
 
 def kernel(
     sections, batches, shards,
-    tokens, chosen, gain, router, freq, w_q, w_k, w_v, w_o,
+    tokens_hbm, chosen_hbm, gain_hbm, router, w_q, w_k, w_v, w_o,
     out,
-    w_in, w_back, picks, next_pick, picked, raw_rows, arrived, normed, spread,
-    compact, part, joint, attended, both, slot_att, out_part, returned,
+    tokens, chosen, gain, w_in, w_back, inverse, inverse_in, picks, next_pick, picked, raw_rows, arrived, normed, spread,
+    compact, part, joint, attended, both, slot_att, out_part, middle, returned,
     w_sem, pick_send, pick_recv, row_send, row_recv, sp_send, sp_recv,
-    jt_send, jt_recv, at_send, at_recv, rt_send, rt_recv,
+    fw_send, jt_send, jt_recv, at_send, at_recv, md_send, md_recv, rt_send, rt_recv,
 ):
     z, g, t = lax.axis_index("section"), lax.axis_index("dp"), lax.axis_index("seq")
     plane = batches * shards
     me = g * shards + t
+    pair = 2 if shards % 2 == 0 else 1
+    rows_of = shards // pair
+    core, row = lax.rem(t, pair), lax.div(t, pair)
+    sibling = (z, g, row * pair + lax.rem(core + 1, pair))
     after = (lax.rem(z + 1, sections), g, t)
     before = (lax.rem(z + sections - 1, sections), g, t)
     tok_dev, width = tokens.shape
@@ -91,7 +95,12 @@
         pltpu.make_async_copy(w, w_in.at[i], w_sem.at[i]) for i, w in enumerate((w_q, w_k, w_v))
     ]
     loads.append(pltpu.make_async_copy(w_o, w_back, w_sem.at[3]))
-    for load in loads:
+    early = [
+        pltpu.make_async_copy(chosen_hbm, chosen, w_sem.at[4]),
+        pltpu.make_async_copy(tokens_hbm, tokens, w_sem.at[5]),
+        pltpu.make_async_copy(gain_hbm, gain, w_sem.at[6]),
+    ]
+    for load in early + loads:
         load.start()
 
     def peer(step):
@@ -116,6 +125,7 @@
     def _(step):
         pl.semaphore_signal(barrier, inc=1, device_id=peer(step)[1], device_id_type=MESH)
 
+    early[0].wait()
     my_picks = chosen[...]
     pick_cols = picks.shape[2]
     padded = my_picks
@@ -142,39 +152,72 @@
     lowest = t * tok_dev
     by_slot, by_row = local_onehots(next_pick[0:1, :count], lowest, slots, tok_dev)
     gather = nt_dot(by_slot, by_row).astype(BF16)
-    picked[...] = nn_dot(gather, tokens[...]).astype(BF16)
-    row_copy = remote(picked, raw_rows, row_send.at[0], row_recv.at[0], after)
-    row_copy.start()
-
-    angles = as_column(my_picks.astype(F32)) * freq[...]
+    early[1].wait()
+    chosen_rows = nn_dot(gather, tokens[...])
+    inverse[...] = jnp.broadcast_to(
+        lax.rsqrt(jnp.mean(chosen_rows * chosen_rows, axis=1, keepdims=True) + EPSILON),
+        inverse.shape,
+    )
+    inverse_copy = remote(
+        inverse, inverse_in, row_send.at[batches + 1], row_recv.at[batches + 1], after
+    )
+    inverse_copy.start()
+    for b in range(batches):
+        picked[b] = chosen_rows[:, b * depth : (b + 1) * depth].astype(BF16)
+
+    def row_copy(step):
+        b = mate(step)[0]
+        return remote(picked.at[b], raw_rows.at[b], row_send.at[step], row_recv.at[step], after)
+
+    order = [step % batches for step in range(1, batches + 1)]
+    for step in order:
+        row_copy(step).start()
+
+    lane = lax.broadcasted_iota(jnp.int32, (count, HD), 1)
+    twin = jnp.where(lane < HD // 2, lane, lane - HD // 2).astype(F32)
+    angles = as_column(my_picks.astype(F32)) * jnp.exp(twin * (-2.0 / HD * np.log(ROPE_BASE)))
     cosine = jnp.cos(angles)
-    lane = lax.broadcasted_iota(jnp.int32, (count, HD), 1)
     sine = jnp.where(lane < HD // 2, -1.0, 1.0) * jnp.sin(angles)
-
-    row_copy.wait_recv()
-    relay = remote(tokens, arrived, row_send.at[1], row_recv.at[1], after)
+    early[2].wait()
+
+    def spread_copy(step, turn):
+        b = mate(step)[0]
+        far = lax.rem(row + turn, rows_of)
+        return remote(
+            normed.at[b], spread.at[me], sp_send.at[b * rows_of + far], sp_recv.at[me],
+            (z, b, far * pair + core),
+        )
+
+    def forward_copy(source):
+        return remote(
+            spread.at[source], spread.at[source], fw_send.at[source], sp_recv.at[source], sibling
+        )
+
+    inverse_copy.wait_recv()
+    inv_scale = inverse_in[:, 0:1]
+    for step in order:
+        row_copy(step).wait_recv()
+        b = mate(step)[0]
+        at = pl.ds(pl.multiple_of(b * depth, 128), depth)
+        normed[b] = (raw_rows[b].astype(F32) * inv_scale * gain[:, at]).astype(BF16)
+        if step == 0:
+            spread[me] = normed[g]
+            if pair == 2:
+                forward_copy(me).start()
+
+        @pl.loop(1 if step == 0 else 0, rows_of)
+        def _(turn):
+            spread_copy(step, turn).start()
+
+    relay = remote(tokens, arrived, row_send.at[batches], row_recv.at[batches], after)
     relay.start()
-    rows = raw_rows[...].astype(F32)
-    inv_scale = lax.rsqrt(jnp.mean(rows * rows, axis=1, keepdims=True) + EPSILON)
-    scaled = (rows * inv_scale * gain[...]).astype(BF16)
+    logits = jnp.zeros((slots, 1), F32)
     for b in range(batches):
-        normed[b] = scaled[:, b * depth : (b + 1) * depth]
-
-    def spread_copy(step):
-        index, device = peer(step)
-        return remote(
-            normed.at[lax.div(index, shards)], spread.at[me],
-            sp_send.at[index], sp_recv.at[me], device,
-        )
-
-    @pl.loop(1, plane)
-    def _(step):
-        spread_copy(step).start()
-
-    spread[me] = normed[g]
-    gate = jax.nn.sigmoid(
-        jnp.sum(rows * router[...].astype(F32), axis=1, keepdims=True)
-    )
+        logits = logits + jnp.sum(
+            raw_rows[b].astype(F32) * router[:, b * depth : (b + 1) * depth].astype(F32),
+            axis=1, keepdims=True,
+        )
+    gate = jax.nn.sigmoid(logits)
 
     def arrived_from(buffer, sems, index):
         remote(buffer.at[index], buffer.at[index], sems.at[index], sems.at[index], after).wait_recv()
@@ -184,9 +227,26 @@
     flats = [flat_slots(picks[b, 0:1, :count], shards, slots, tok_dev) for b in range(batches)]
     flat_cols = [as_column(flat) for flat in flats]
 
-    @pl.loop(1, plane)
+    half = batches * rows_of
+
+    def same_core(step):
+        index = lax.rem(g * rows_of + row + step, half)
+        return lax.div(index, rows_of), lax.rem(index, rows_of)
+
+    @pl.loop(1, half)
     def _(step):
-        arrived_from(spread, sp_recv, peer(step)[0])
+        b, far = same_core(step)
+        source = b * shards + far * pair + core
+        arrived_from(spread, sp_recv, source)
+        if pair == 2:
+            forward_copy(source).start()
+
+    if pair == 2:
+
+        @pl.loop(0, half)
+        def _(step):
+            b, far = same_core(step)
+            arrived_from(spread, sp_recv, b * shards + far * pair + 1 - core)
 
     for b in range(batches):
         choose = ones_where(flat_cols[b] == iota_f32((count, shards * slots), 1))
@@ -253,11 +313,39 @@
     both[g] = attended[...]
     loads[3].wait()
 
-    def return_copy(index):
-        device = (z, lax.div(index, shards), lax.rem(index, shards))
+    def middle_copy(batch, far):
+        index = batch * shards + far * pair + 1 - core
+        slot = batch * rows_of + far
         return remote(
-            out_part.at[index], returned.at[me], rt_send.at[index], rt_recv.at[me], device
-        )
+            out_part.at[index], middle.at[slot], md_send.at[slot], md_recv.at[slot], sibling
+        )
+
+    def return_copy(batch, far):
+        place = far * pair + core
+        return remote(
+            out_part.at[batch * shards + place], returned.at[g * rows_of + row],
+            rt_send.at[batch * rows_of + far], rt_recv.at[g * rows_of + row], (z, batch, place),
+        )
+
+    def send_sums(step):
+        batch = mate(step)[0]
+
+        @pl.loop(0, rows_of)
+        def _(turn):
+            far = lax.rem(row + 1 + turn, rows_of)
+            index = batch * shards + far * pair + core
+            if pair == 2:
+                arrived_from(middle, md_recv, batch * rows_of + far)
+                out_part[index] = (
+                    out_part[index].astype(F32) + middle[batch * rows_of + far].astype(F32)
+                ).astype(BF16)
+            if step:
+                return_copy(batch, far).start()
+            else:
+
+                @pl.when(turn < rows_of - 1)
+                def _():
+                    return_copy(batch, far).start()
 
     out_cols = min(256, depth)
     for step in range(batches):
@@ -278,43 +366,60 @@
                     owner * slots : (owner + 1) * slots
                 ]
 
-        @pl.loop(1 if step == 0 else 0, shards)
-        def _(turn):
-            return_copy(batch * shards + lax.rem(t + turn, shards)).start()
-
-    returned[me] = out_part[me]
+        if pair == 2:
+
+            @pl.loop(0, rows_of)
+            def _(turn):
+                middle_copy(batch, lax.rem(row + 1 + turn, rows_of)).start()
+
+        if step:
+            send_sums(step - 1)
+    send_sums(batches - 1)
+    returned[g * rows_of + row] = out_part[me]
     by_slot, by_row = local_onehots(my_picks, lowest, slots, tok_dev)
     scatter = nt_dot(by_row, by_slot).astype(BF16)
     held = jnp.sum(by_row.astype(F32), axis=1, keepdims=True) > 0.5
     relay.wait_recv()
 
-    @pl.loop(1, plane)
+    @pl.loop(1, half)
     def _(step):
-        arrived_from(returned, rt_recv, peer(step)[0])
+        b, far = same_core(step)
+        arrived_from(returned, rt_recv, b * rows_of + far)
 
     for b in range(batches):
         at = slice(b * depth, (b + 1) * depth)
-        delta = returned[b * shards].astype(F32)
-        for owner in range(1, shards):
-            delta = delta + returned[b * shards + owner].astype(F32)
+        delta = returned[b * rows_of].astype(F32)
+        for far in range(1, rows_of):
+            delta = delta + returned[b * rows_of + far].astype(F32)
         delta = delta.astype(BF16).astype(F32)
-        updated = (raw_rows[:, at].astype(F32) + gate * delta).astype(BF16)
+        updated = (raw_rows[b].astype(F32) + gate * delta).astype(BF16)
         replaced = nn_dot(scatter, updated)
         out[:, at] = jnp.where(held, replaced, arrived[:, at].astype(F32)).astype(BF16)
 
     pick_back.wait_send()
-    row_copy.wait_send()
+    inverse_copy.wait_send()
     relay.wait_send()
+    for step in range(batches):
+        row_copy(step).wait_send()
+
+        @pl.loop(1 if step == 0 else 0, rows_of)
+        def _(turn):
+            spread_copy(step, turn).wait_send()
+            return_copy(mate(step)[0], lax.rem(row + turn, rows_of)).wait_send()
+
     for step in range(1, batches):
         pick_copy(step).wait_send()
         attended_copy(step).wait_send()
         for which in range(3):
             joint_copy(step, which).wait_send()
 
-    @pl.loop(1, plane)
-    def _(step):
-        spread_copy(step).wait_send()
-        return_copy(peer(step)[0]).wait_send()
+    if pair == 2:
+
+        @pl.loop(0, half)
+        def _(step):
+            b, far = same_core(step)
+            forward_copy(b * shards + far * pair + core).wait_send()
+            middle_copy(b, far).wait_send()
 
 
 def per_device(incoming, chosen, norm_gain, router, w_query, w_key, w_value, w_out_t):
@@ -326,9 +431,8 @@
     count = chosen.shape[2]
     slots = tok_dev // 4
     depth, head_cols = w_query.shape[1:]
-    half = np.arange(HD // 2, dtype=np.float32)
-    freq = np.float32(ROPE_BASE) ** (np.float32(-2.0) * half / np.float32(HD))
-    freq = jnp.asarray(np.concatenate([freq, freq])[None].astype(np.float32))
+    pair = 2 if shards % 2 == 0 else 1
+    half = batches * (shards // pair)
     pick_cols = -(-count // 128) * 128
     vmem = pl.BlockSpec(memory_space=pltpu.VMEM)
     hbm = pl.BlockSpec(memory_space=pl.ANY)
@@ -336,15 +440,20 @@
     result = pl.pallas_call(
         functools.partial(kernel, sections, batches, shards),
         out_shape=jax.ShapeDtypeStruct((tok_dev, width), BF16),
-        in_specs=[vmem] * 5 + [hbm] * 4,
+        in_specs=[hbm] * 3 + [vmem] + [hbm] * 4,
         out_specs=vmem,
         scratch_shapes=[
+            pltpu.VMEM((tok_dev, width), BF16),
+            pltpu.VMEM((1, count), jnp.int32),
+            pltpu.VMEM((1, width), F32),
             pltpu.VMEM((3, depth, head_cols), BF16),
             pltpu.VMEM((depth, head_cols), BF16),
+            pltpu.VMEM((slots, 128), F32),
+            pltpu.VMEM((slots, 128), F32),
             pltpu.VMEM((batches, 8, pick_cols), jnp.int32),
             pltpu.VMEM((8, pick_cols), jnp.int32),
-            pltpu.VMEM((slots, width), BF16),
-            pltpu.VMEM((slots, width), BF16),
+            pltpu.VMEM((batches, slots, depth), BF16),
+            pltpu.VMEM((batches, slots, depth), BF16),
             pltpu.VMEM((tok_dev, width), BF16),
             pltpu.VMEM((batches, slots, depth), BF16),
             pltpu.VMEM((plane, slots, depth), BF16),
@@ -355,20 +464,21 @@
             pltpu.VMEM((batches, count, head_cols), BF16),
             pltpu.VMEM((shards * slots, head_cols), BF16),
             pltpu.VMEM((plane, slots, depth), BF16),
-            pltpu.VMEM((plane, slots, depth), BF16),
-            dma((4,)),
+            pltpu.VMEM((half, slots, depth), BF16),
+            pltpu.VMEM((half, slots, depth), BF16),
+            dma((7,)),
             dma((batches,)), dma((batches + 1,)),
-            dma((2,)), dma((2,)),
-            dma((plane,)), dma((plane,)),
+            dma((batches + 2,)), dma((batches + 2,)),
+            dma((half,)), dma((plane,)), dma((plane,)),
             dma((batches, 3)), dma((batches, 3)),
             dma((batches,)), dma((batches,)),
-            dma((plane,)), dma((plane,)),
+            dma((half,)), dma((half,)), dma((half,)), dma((half,)),
         ],
         compiler_params=pltpu.CompilerParams(
             collective_id=0, has_side_effects=True, vmem_limit_bytes=52 * 1024 * 1024
         ),
     )(
-        incoming[0, 0], chosen[0], norm_gain, router, freq,
+        incoming[0, 0], chosen[0], norm_gain, router,
         w_query[0], w_key[0], w_value[0], w_out_t[0],
     )
     return result[None, None]

time: 68.7 us -> 58.6 us (0.85)
  Pallas kernels: 64.6 us -> 54.6 us
    pallas_call x1, Pallas kernels: 64.6 us -> 54.6 us  [per_device(): pl.pallas_call(functools.partial(kernel, sections, batches, shards), out_...]
    unnamed x9 -> x7, local copies, waits for them, and re-layouts: 3.72 us -> 3.06 us
where the time goes in v3:
time: 58.6 us; the launch traced here: 57.7 us
  Pallas kernels  54.6 us (93%)
  local copies, waits for them, and re-layouts  3.06 us (5%)
    pallas_call x1, Pallas kernels, per_device(): pl.pallas_call(functools.partial(kernel, sections, batches, shards), out_...  54.6 us
    unnamed x7, local copies, waits for them, and re-layouts  3.06 us

profile of v3, /device:TPU:1, one launch (start us, length us, event | category | flops | bytes accessed | tf_op | source)
XLA Modules:
  0.0 57.7 jit_solution(1585618945941163558)
XLA Ops:
  0.0 0.0 copy-start
  0.0 0.7 %copy-done = f32[1,4096]{1,0:T(1,128)S(1)} copy-done((f32[1,4096]{1,0:T(1,128)S(1)}, f32[1,4096]{1,0:T(1,128)}, u32[]{:S(2)}) %copy-start) | copy-done | bytes 16408
  0.7 0.0 copy-start.1
  0.7 0.7 %copy-done.1 = bf16[1,4096]{1,0:T(2,128)(2,1)S(1)} copy-done((bf16[1,4096]{1,0:T(2,128)(2,1)S(1)}, bf16[1,4096]{1,0:T(2,128)(2,1)}, u32[]{:S(2)}) %copy-start.1) | copy-done | bytes 8216
  1.4 0.0 copy-start.2
  1.4 0.7 %copy-done.2 = s32[1,1,64]{2,1,0:T(1,128)S(1)} copy-done((s32[1,1,64]{2,1,0:T(1,128)S(1)}, s32[1,1,64]{2,1,0:T(1,128)}, u32[]{:S(2)}) %copy-start.2) | copy-done | bytes 280
  2.1 54.6 %shard_map.82 = bf16[128,4096]{1,0:T(8,128)(2,1)S(1)} custom-call(bf16[128,4096]{1,0:T(8,128)(2,1)} %bitcast.13, s32[1,64]{1,0:T(1,128)S(1)} %bitcast.8, f32[1,4096]{1,0:T(1,128)S(1)} %copy-done, bf16[1,4096]{1,0:T(2,128)(2,1)S(1)} %copy-done.1, bf16[2048,1024]{1,0:T(8,128)(2,1)} %bitcast.9, bf16[2048,1024]{1,0:T(8,128)(2,1)} %bitcast.10, ...), custom_call_target="tpu_custom_call" | custom-call | tf_op jit(solution)/shard_map/pallas_call | solution.py:440
  56.7 1.0 %copy.10 = bf16[1,1,128,4096]{3,2,1,0:T(8,128)(2,1)} copy(bf16[1,1,128,4096]{3,2,1,0:T(8,128)(2,1)S(1)} %bitcast.7) | data formatting | bytes 2097152
Async XLA Ops:
  0.0 0.7 %copy-start = (f32[1,4096]{1,0:T(1,128)S(1)}, f32[1,4096]{1,0:T(1,128)}, u32[]{:S(2)}) copy-start(f32[1,4096]{1,0:T(1,128)} %gain_hbm.1) | copy-start | bytes 49156
  0.7 0.7 %copy-start.1 = (bf16[1,4096]{1,0:T(2,128)(2,1)S(1)}, bf16[1,4096]{1,0:T(2,128)(2,1)}, u32[]{:S(2)}) copy-start(bf16[1,4096]{1,0:T(2,128)(2,1)} %router.1) | copy-start | bytes 24580
  1.4 0.7 %copy-start.2 = (s32[1,1,64]{2,1,0:T(1,128)S(1)}, s32[1,1,64]{2,1,0:T(1,128)}, u32[]{:S(2)}) copy-start(s32[1,1,64]{2,1,0:T(1,128)} %param.9) | copy-start | bytes 772

commit v4 on v3

--- a/solution.py
+++ b/solution.py
@@ -70,9 +70,9 @@
 
 def kernel(
     sections, batches, shards,
-    tokens_hbm, chosen_hbm, gain_hbm, router, w_q, w_k, w_v, w_o,
+    tokens_hbm, chosen_hbm, gain_hbm, router_hbm, w_q, w_k, w_v, w_o,
     out,
-    tokens, chosen, gain, w_in, w_back, inverse, inverse_in, picks, next_pick, picked, raw_rows, arrived, normed, spread,
+    tokens, chosen, gain, router, w_in, w_back, inverse, inverse_in, picks, next_pick, picked, raw_rows, arrived, normed, spread,
     compact, part, joint, attended, both, slot_att, out_part, middle, returned,
     w_sem, pick_send, pick_recv, row_send, row_recv, sp_send, sp_recv,
     fw_send, jt_send, jt_recv, at_send, at_recv, md_send, md_recv, rt_send, rt_recv,
@@ -99,6 +99,7 @@
         pltpu.make_async_copy(chosen_hbm, chosen, w_sem.at[4]),
         pltpu.make_async_copy(tokens_hbm, tokens, w_sem.at[5]),
         pltpu.make_async_copy(gain_hbm, gain, w_sem.at[6]),
+        pltpu.make_async_copy(router_hbm, router, w_sem.at[7]),
     ]
     for load in early + loads:
         load.start()
@@ -211,6 +212,7 @@
 
     relay = remote(tokens, arrived, row_send.at[batches], row_recv.at[batches], after)
     relay.start()
+    early[3].wait()
     logits = jnp.zeros((slots, 1), F32)
     for b in range(batches):
         logits = logits + jnp.sum(
@@ -253,41 +255,40 @@
         source = spread[b * shards : (b + 1) * shards].reshape(shards * slots, depth)
         compact[b * count : (b + 1) * count, :] = nn_dot(choose, source).astype(BF16)
 
-    cols = min(256, head_cols)
-
-    def joint_copy(step, which):
+    pieces, cols = part.shape[1], head_cols // part.shape[1]
+
+    def joint_copy(step, piece):
         index, device = mate(step)
         return remote(
-            part.at[index, which], joint.at[g, which],
-            jt_send.at[step, which], jt_recv.at[g, which], device,
-        )
+            part.at[index, piece], joint.at[g, piece],
+            jt_send.at[step, piece], jt_recv.at[g, piece], device,
+        )
+
+    def attended_copy(step, piece):
+        device = mate(step)[1]
+        return remote(
+            attended.at[piece], both.at[g, piece],
+            at_send.at[step, piece], at_recv.at[g, piece], device,
+        )
+
+    def arrived_piece(buffer, sems, index, piece):
+        slot, sem = buffer.at[index, piece], sems.at[index, piece]
+        remote(slot, slot, sem, sem, after).wait_recv()
 
     for which in range(3):
         loads[which].wait()
 
-        @pl.loop(0, head_cols // cols)
-        def _(block):
-            at = pl.ds(pl.multiple_of(block * cols, cols), cols)
+    @pl.loop(0, pieces)
+    def _(piece):
+        for which in range(3):
+            at = pl.ds(pl.multiple_of(piece * cols, cols), cols)
             product = nn_dot(compact[...], w_in[which, :, at]).astype(BF16)
             for b in range(batches):
-                part[b, which, :, at] = product[b * count : (b + 1) * count]
-
+                part[b, piece, :, which * cols : (which + 1) * cols] = product[
+                    b * count : (b + 1) * count
+                ]
         for step in range(1, batches):
-            joint_copy(step, which).start()
-        joint[g, which] = part[g, which]
-
-    summed = []
-    for which in range(3):
-        for step in range(1, batches):
-            index = mate(step)[0]
-            slot = joint.at[index, which]
-            remote(
-                slot, slot, jt_recv.at[index, which], jt_recv.at[index, which], after
-            ).wait_recv()
-        total = joint[0, which].astype(F32)
-        for b in range(1, batches):
-            total = total + joint[b, which].astype(F32)
-        summed.append(total)
+            joint_copy(step, piece).start()
 
     def rope(value):
         swapped = jnp.concatenate([value[:, HD // 2 :], value[:, : HD // 2]], axis=1)
@@ -296,21 +297,28 @@
     causal = lax.broadcasted_iota(jnp.int32, (count, count), 1) <= lax.broadcasted_iota(
         jnp.int32, (count, count), 0
     )
-    for head in range(head_cols // HD):
-        at = slice(head * HD, (head + 1) * HD)
-        scores = nt_dot(rope(summed[0][:, at]), rope(summed[1][:, at])) * HD ** (-0.5)
-        scores = jnp.where(causal, scores, NEG_FILL)
-        exponent = jnp.exp(scores - jnp.max(scores, axis=1, keepdims=True))
-        weights = (exponent / jnp.sum(exponent, axis=1, keepdims=True)).astype(BF16)
-        attended[:, at] = nn_dot(weights, summed[2][:, at].astype(BF16)).astype(BF16)
-
-    def attended_copy(step):
-        index, device = mate(step)
-        return remote(attended, both.at[g], at_send.at[step], at_recv.at[g], device)
-
-    for step in range(1, batches):
-        attended_copy(step).start()
-    both[g] = attended[...]
+    for piece in range(pieces):
+        total = part[g, piece].astype(F32)
+        for step in range(1, batches):
+            index = mate(step)[0]
+            arrived_piece(joint, jt_recv, index, piece)
+            total = total + joint[index, piece].astype(F32)
+        for head in range(cols // HD):
+            query, key, value = (
+                total[:, which * cols + head * HD : which * cols + (head + 1) * HD]
+                for which in range(3)
+            )
+            scores = nt_dot(rope(query), rope(key)) * HD ** (-0.5)
+            scores = jnp.where(causal, scores, NEG_FILL)
+            exponent = jnp.exp(scores - jnp.max(scores, axis=1, keepdims=True))
+            weights = (exponent / jnp.sum(exponent, axis=1, keepdims=True)).astype(BF16)
+            attended[piece, :, head * HD : (head + 1) * HD] = nn_dot(
+                weights, value.astype(BF16)
+            ).astype(BF16)
+        for step in range(1, batches):
+            attended_copy(step, piece).start()
+        both[g, piece] = attended[piece]
+
     loads[3].wait()
 
     def middle_copy(batch, far):
@@ -350,11 +358,14 @@
     out_cols = min(256, depth)
     for step in range(batches):
         batch = mate(step)[0]
-        if step:
-            arrived_from(both, at_recv, batch)
         place = flat_slots(picks[batch, 0:1, :count], shards, slots, tok_dev)
         place = ones_where(place == iota_f32((shards * slots, count), 0))
-        slot_att[...] = nn_dot(place, both[batch]).astype(BF16)
+        for piece in range(pieces):
+            if step:
+                arrived_piece(both, at_recv, batch, piece)
+            slot_att[:, piece * cols : (piece + 1) * cols] = nn_dot(
+                place, both[batch, piece]
+            ).astype(BF16)
 
         @pl.loop(0, depth // out_cols)
         def _(block):
@@ -381,13 +392,14 @@
     held = jnp.sum(by_row.astype(F32), axis=1, keepdims=True) > 0.5
     relay.wait_recv()
 
-    @pl.loop(1, half)
-    def _(step):
-        b, far = same_core(step)
-        arrived_from(returned, rt_recv, b * rows_of + far)
-
-    for b in range(batches):
-        at = slice(b * depth, (b + 1) * depth)
+    for step in range(batches):
+        b = mate(step)[0]
+
+        @pl.loop(1 if step == 0 else 0, rows_of)
+        def _(turn):
+            arrived_from(returned, rt_recv, b * rows_of + lax.rem(row + turn, rows_of))
+
+        at = pl.ds(pl.multiple_of(b * depth, 128), depth)
         delta = returned[b * rows_of].astype(F32)
         for far in range(1, rows_of):
             delta = delta + returned[b * rows_of + far].astype(F32)
@@ -409,9 +421,9 @@
 
     for step in range(1, batches):
         pick_copy(step).wait_send()
-        attended_copy(step).wait_send()
-        for which in range(3):
-            joint_copy(step, which).wait_send()
+        for piece in range(pieces):
+            attended_copy(step, piece).wait_send()
+            joint_copy(step, piece).wait_send()
 
     if pair == 2:
 
@@ -433,6 +445,8 @@
     depth, head_cols = w_query.shape[1:]
     pair = 2 if shards % 2 == 0 else 1
     half = batches * (shards // pair)
+    pieces = max(1, head_cols // 256)
+    cols = head_cols // pieces
     pick_cols = -(-count // 128) * 128
     vmem = pl.BlockSpec(memory_space=pltpu.VMEM)
     hbm = pl.BlockSpec(memory_space=pl.ANY)
@@ -440,12 +454,13 @@
     result = pl.pallas_call(
         functools.partial(kernel, sections, batches, shards),
         out_shape=jax.ShapeDtypeStruct((tok_dev, width), BF16),
-        in_specs=[hbm] * 3 + [vmem] + [hbm] * 4,
+        in_specs=[hbm] * 8,
         out_specs=vmem,
         scratch_shapes=[
             pltpu.VMEM((tok_dev, width), BF16),
             pltpu.VMEM((1, count), jnp.int32),
             pltpu.VMEM((1, width), F32),
+            pltpu.VMEM((1, width), BF16),
             pltpu.VMEM((3, depth, head_cols), BF16),
             pltpu.VMEM((depth, head_cols), BF16),
             pltpu.VMEM((slots, 128), F32),
@@ -458,24 +473,24 @@
             pltpu.VMEM((batches, slots, depth), BF16),
             pltpu.VMEM((plane, slots, depth), BF16),
             pltpu.VMEM((batches * count, depth), BF16),
-            pltpu.VMEM((batches, 3, count, head_cols), BF16),
-            pltpu.VMEM((batches, 3, count, head_cols), BF16),
-            pltpu.VMEM((count, head_cols), BF16),
-            pltpu.VMEM((batches, count, head_cols), BF16),
+            pltpu.VMEM((batches, pieces, count, 3 * cols), BF16),
+            pltpu.VMEM((batches, pieces, count, 3 * cols), BF16),
+            pltpu.VMEM((pieces, count, cols), BF16),
+            pltpu.VMEM((batches, pieces, count, cols), BF16),
             pltpu.VMEM((shards * slots, head_cols), BF16),
             pltpu.VMEM((plane, slots, depth), BF16),
             pltpu.VMEM((half, slots, depth), BF16),
             pltpu.VMEM((half, slots, depth), BF16),
-            dma((7,)),
+            dma((8,)),
             dma((batches,)), dma((batches + 1,)),
             dma((batches + 2,)), dma((batches + 2,)),
             dma((half,)), dma((plane,)), dma((plane,)),
-            dma((batches, 3)), dma((batches, 3)),
-            dma((batches,)), dma((batches,)),
+            dma((batches, pieces)), dma((batches, pieces)),
+            dma((batches, pieces)), dma((batches, pieces)),
             dma((half,)), dma((half,)), dma((half,)), dma((half,)),
         ],
         compiler_params=pltpu.CompilerParams(
-            collective_id=0, has_side_effects=True, vmem_limit_bytes=52 * 1024 * 1024
+            collective_id=0, has_side_effects=True, vmem_limit_bytes=64 * 1024 * 1024
         ),
     )(
         incoming[0, 0], chosen[0], norm_gain, router,

time: 58.6 us -> 54.4 us (0.928)
  Pallas kernels: 54.6 us -> 51 us
  local copies, waits for them, and re-layouts: 3.06 us -> 2.29 us
    pallas_call x1, Pallas kernels: 54.6 us -> 51 us  [per_device(): pl.pallas_call(functools.partial(kernel, sections, batches, shards), out_...]
    unnamed x7 -> x1, local copies, waits for them, and re-layouts: 3.06 us -> 2.29 us
where the time goes in v4:
time: 54.4 us; the launch traced here: 53.3 us
  Pallas kernels  51 us (94%)
  local copies, waits for them, and re-layouts  2.29 us (4%)
    pallas_call x1, Pallas kernels, per_device(): pl.pallas_call(functools.partial(kernel, sections, batches, shards), out_...  51 us
    unnamed x1, local copies, waits for them, and re-layouts  2.29 us

profile of v4, /device:TPU:1, one launch (start us, length us, event | category | flops | bytes accessed | tf_op | source)
XLA Modules:
  0.0 53.3 jit_solution(12163027898172337922)
XLA Ops:
  0.0 51.0 %shard_map.82 = bf16[128,4096]{1,0:T(8,128)(2,1)} custom-call(bf16[128,4096]{1,0:T(8,128)(2,1)} %bitcast.12, s32[1,64]{1,0:T(1,128)} %bitcast.13, f32[1,4096]{1,0:T(1,128)} %gain_hbm.1, bf16[1,4096]{1,0:T(2,128)(2,1)} %router_hbm.1, bf16[2048,1024]{1,0:T(8,128)(2,1)} %bitcast.7, bf16[2048,1024]{1,0:T(8,128)(2,1)} %bitcast.8, bf16[2048,1024]{1,0:T(8,128)(2,1)} %bitcast.9, ...), custom_call_target="tpu_custom_call" | custom-call | tf_op jit(solution)/shard_map/pallas_call | solution.py:454
  51.0 2.3 %copy.10 = bf16[1,1,128,4096]{3,2,1,0:T(8,128)(2,1)} copy(bf16[1,1,128,4096]{3,2,1,0:T(8,128)(2,1)} %bitcast.11) | data formatting | bytes 2097152
